TPU v7x, 256 devices: a whole 4x4x8 slice. The times are simulated.
256 devices in a mesh: section: 16 (over z, x_hi), dp: 16 (over x_lo, y, core).
Axes of the slice: x: 4 (x_hi: 2, x_lo: 2; x = x_hi * 2 + x_lo), y: 4, z: 8, core: 2. Of those that a mesh axis runs over, the one named last changes fastest.
Arguments:
- section_input: bfloat16 [16, 2048, 12288], P('section', 'dp'), may hold values from -0.19921875 to 0.19921875
- boundary_grad: bfloat16 [16, 2048, 12288], P('section', 'dp'), may hold values from -6 to 6
- carry_error: bfloat16 [16, 2048, 12288], P('section', 'dp'), may hold values from -4 to 4
- act_basis: bfloat16 [16, 12288, 64], P('section', 'dp'), may hold values from -6 to 6
- weight_basis: bfloat16 [16, 12288, 128], P('section', 'dp'), may hold values from -6 to 6
- outside_left: bfloat16 [2048, 64], P('dp'), may hold values from -1 to 1
- outside_right: bfloat16 [16, 12288, 64], P('dp', 'section'), may hold values from -6 to 6
Outputs:
- new_error: bfloat16 [16, 2048, 12288], P('section', 'dp')
- weight_left: bfloat16 [16, 12288, 128], P('section', 'dp')
- weight_right: bfloat16 [16, 12288, 128], P('section', 'dp')
All inputs are finite; a program needn't handle non-finite values.
Results may differ from a plain program's by a relative error of at most 0.03.
Values may be sent and summed in bfloat16 or wider, within the bound.
No kernel may reach another device: no remote copies, remote signals or barrier semaphores. Data moves between devices by JAX's collectives and lax.ppermute only.
A program may use at most 64 MiB of HBM per device.

v0:
```python
import jax
import jax.numpy as jnp
from jax import lax
from jax.sharding import PartitionSpec as P


def from_behind(value, axis, steps):
    count = lax.axis_size(axis)
    initial, last = (max(0, -steps), min(count, count - steps))
    return lax.ppermute(value, axis, [(source, source + steps) for source in range(initial, last)])


def orthonormal(block):
    gram = jnp.dot(
        block.T, block, precision=lax.Precision.HIGHEST, preferred_element_type=jnp.float32
    )
    factor = jnp.linalg.cholesky(gram)
    return jax.scipy.linalg.solve_triangular(factor, block.T, lower=True).T


def body(
    section_input, boundary_grad, carry_error, act_basis, weight_basis, outside_left, outside_right
):
    inputs = section_input[0]
    width = inputs.shape[1]
    bases = (
        lax.all_gather(act_basis, "dp", axis=1, tiled=True),
        lax.all_gather(weight_basis, "dp", axis=1, tiled=True),
    )
    basis_a = bases[0][0]
    basis_w = bases[1][0]
    merged = boundary_grad[0].astype(jnp.float32) + carry_error[0].astype(jnp.float32)
    proj = jnp.dot(merged, basis_a.astype(jnp.float32), precision=lax.Precision.HIGHEST)
    left = orthonormal(proj).astype(jnp.bfloat16)
    right = jnp.dot(merged.T, left.astype(jnp.float32), precision=lax.Precision.HIGHEST).astype(
        jnp.bfloat16
    )
    rebuilt = jnp.dot(left, right.T, preferred_element_type=jnp.float32)
    new_error = (merged - rebuilt).astype(jnp.bfloat16)[None]
    recv_left, recv_right = from_behind((left, right), "section", -1)
    beyond = lax.all_gather(outside_right, "section", axis=1, tiled=True)[0]
    is_last = lax.axis_index("section") == lax.axis_size("section") - 1
    recv_left = jnp.where(is_last, outside_left, recv_left)
    recv_right = jnp.where(is_last, beyond, recv_right)
    inner = jnp.dot(recv_right.T, basis_w, preferred_element_type=jnp.float32).astype(jnp.bfloat16)
    core = jnp.dot(inputs.T, recv_left, preferred_element_type=jnp.float32).astype(jnp.bfloat16)
    share_rows = width // lax.axis_size("dp")
    partial_value = (
        jnp.dot(core, inner, preferred_element_type=jnp.float32)
        .astype(jnp.bfloat16)
        .astype(jnp.float32)
    )
    summed = lax.psum(partial_value.astype(jnp.bfloat16), "dp").astype(jnp.float32)
    factor = orthonormal(summed).astype(jnp.bfloat16)
    first = jnp.dot(inputs, factor, preferred_element_type=jnp.float32)
    second = jnp.dot(
        recv_left.astype(jnp.float32).T, first, precision=lax.Precision.HIGHEST
    ).astype(jnp.bfloat16)
    term = (
        jnp.dot(recv_right, second, preferred_element_type=jnp.float32)
        .astype(jnp.bfloat16)
        .astype(jnp.float32)
    )
    total = lax.psum(term.astype(jnp.bfloat16), "dp").astype(jnp.float32)
    start = lax.axis_index("dp") * share_rows
    weight_left = lax.dynamic_slice_in_dim(factor, start, share_rows, 0)
    weight_right = lax.dynamic_slice_in_dim(total, start, share_rows, 0).astype(jnp.bfloat16)
    return (new_error, weight_left[None], weight_right[None])


def solution(mesh):
    return jax.shard_map(
        body,
        mesh=mesh,
        in_specs=(
            P("section", "dp", None),
            P("section", "dp", None),
            P("section", "dp", None),
            P("section", "dp", None),
            P("section", "dp", None),
            P("dp", None),
            P("dp", "section", None),
        ),
        out_specs=(P("section", "dp", None), P("section", "dp", None), P("section", "dp", None)),
        check_vma=False,
    )
```

profile of v0, /device:TPU:1, one launch (start us, length us, event | category | flops | bytes accessed | tf_op | source)
XLA Modules:
  0.0 503.2 jit_solution(8158907087991974384)
XLA Ops:
  7.2 0.0 copy-start
  7.2 0.0 all-gather.4.cloned.1.call-start
  7.2 0.7 all-gather.4.cloned.1.call-update
  7.9 0.0 all-gather.6.cloned.1.call-start
  8.0 0.7 all-gather.6.cloned.1.call-update
  8.7 0.0 all-gather.8.cloned.1.call-start
  8.7 0.7 all-gather.8.cloned.1.call-update
  9.4 0.0 all-reduce.3.cloned.1.call-start
  9.4 40.3 %all-gather.4.cloned.1.call-done = bf16[1,12288,64]{1,2,0:T(8,128)(2,1)} async-done(((bf16[1,768,64]{1,2,0:T(8,128)(2,1)}), bf16[1,12288,64]{1,2,0:T(8,128)(2,1)}) %all-gather.4.cloned.1.call-update) | async-done | bytes 1572880 | tf_op jit(solution)/shard_map/all_gather | solution.py:27
  49.8 7.4 %fusion.3 = f32[128,64]{0,1:T(8,128)S(1)} fusion(bf16[1,128,12288]{2,1,0:T(8,128)(2,1)} %param.9, bf16[1,128,12288]{2,1,0:T(8,128)(2,1)} %param.8, bf16[1,12288,64]{1,2,0:T(8,128)(2,1)} %all-gather.4.cloned.1.call-done), kind=kOutput, calls=%fused_computation.9 | convolution fusion | flops 1212678144 | bytes 7897088 | tf_op jit(solution)/shard_map/dot_general | solution.py:33
  57.2 0.2 fusion.23
  57.4 0.1 copy.10
  57.5 5.8 %cholesky.29 = f32[64,64]{1,0:T(8,128)S(1)} custom-call(f32[64,64]{1,0:T(8,128)S(1)} %fusion.22), custom_call_target="Cholesky" | custom-call | tf_op jit(solution)/shard_map/jit(cholesky)/cholesky | solution.py:17
  63.3 0.6 compare_reduce_fusion.1
  64.0 0.7 fusion.20
  64.6 4.9 custom-call.14
  69.6 0.2 convolution_convert_fusion.6
  69.8 7.4 %convolution_convert_fusion.4 = bf16[12288,64]{0,1:T(8,128)(2,1)} fusion(bf16[128,64]{0,1:T(8,128)(2,1)S(1)} %convolution_convert_fusion.6, bf16[1,128,12288]{2,1,0:T(8,128)(2,1)} %param.9, bf16[1,128,12288]{2,1,0:T(8,128)(2,1)} %param.8), kind=kOutput, calls=%fused_computation.7 | convolution fusion | flops 1213464576 | bytes 7880704 | tf_op jit(solution)/shard_map/dot_general | solution.py:35
  77.2 1.3 collective-permute-start.1
  78.5 0.0 copy-start.3
  78.5 1.3 collective-permute-start
  79.8 59.8 %all-gather.6.cloned.1.call-done = bf16[1,12288,64]{1,2,0:T(8,128)(2,1)} async-done(((bf16[1,768,64]{1,2,0:T(8,128)(2,1)}), bf16[1,12288,64]{1,2,0:T(8,128)(2,1)}) %all-gather.6.cloned.1.call-update) | async-done | bytes 1572880 | tf_op jit(solution)/shard_map/all_gather | solution.py:41
  139.5 0.0 collective-permute-done.1
  139.5 48.2 %all-gather.8.cloned.1.call-done = bf16[1,12288,128]{2,1,0:T(8,128)(2,1)} async-done(((bf16[1,768,128]{2,1,0:T(8,128)(2,1)}), bf16[1,12288,128]{2,1,0:T(8,128)(2,1)}) %all-gather.8.cloned.1.call-update) | async-done | bytes 3145744 | tf_op jit(solution)/shard_map/all_gather | solution.py:28
  187.7 3.6 fusion.13
  191.3 0.0 collective-permute-done
  191.3 0.0 copy-done
  191.3 0.0 copy-done.3
  191.3 3.0 convolution_convert_fusion.2
  194.3 0.0 all-reduce.3.cloned.1.call-update
  194.3 0.2 all-reduce.5.cloned.1.call-start
  194.5 130.3 %all-reduce.3.cloned.1.call-done = bf16[12288,128]{1,0:T(8,128)(2,1)} async-done(((bf16[12288,128]{1,0:T(8,128)(2,1)}), bf16[12288,128]{1,0:T(8,128)(2,1)}) %all-reduce.3.cloned.1.call-update) | async-done | bytes 3145744 | tf_op jit(solution)/shard_map/psum | solution.py:53
  324.9 3.9 fusion.24
  328.7 0.1 copy.11
  328.8 11.7 %cholesky.61 = f32[128,128]{1,0:T(8,128)S(1)} custom-call(f32[128,128]{1,0:T(8,128)S(1)} %fusion.19), custom_call_target="Cholesky" | custom-call | tf_op jit(solution)/shard_map/jit(cholesky)/cholesky | solution.py:17
  340.6 0.6 compare_reduce_fusion
  341.2 0.7 fusion.17
  341.9 9.8 %custom-call.15 = f32[1,128,128]{1,2,0:T(8,128)S(1)} custom-call(f32[1,128,128]{2,1,0:T(8,128)S(1)} %fusion.17), custom_call_target="InvertDiagBlocksLowerTriangular" | custom-call | tf_op jit(solution)/shard_map/jit(_solve_triangular)/triangular_solve | solution.py:18
  351.7 4.2 convolution_convert_fusion.1
  355.9 0.0 copy-start.1
  355.9 0.0 copy-start.2
  356.0 1.1 fusion.7
  357.0 0.5 copy-done.1
  357.6 0.2 convolution_convert_fusion.5
  357.8 0.7 copy-done.2
  358.5 4.1 convolution_convert_fusion
  362.6 0.0 all-reduce.5.cloned.1.call-update
  362.6 6.1 %fusion.1 = bf16[1,128,12288]{2,1,0:T(8,128)(2,1)} fusion(bf16[128,64]{0,1:T(8,128)(2,1)S(1)} %convolution_convert_fusion.6, bf16[12288,64]{0,1:T(8,128)(2,1)} %convolution_convert_fusion.4, bf16[1,128,12288]{2,1,0:T(8,128)(2,1)} %param.9, bf16[1,128,12288]{2,1,0:T(8,128)(2,1)} %param.8), kind=kOutput, calls=%fused_computation.5 | convolution fusion | flops 209190912 | bytes 11026432 | tf_op jit(solution)/shard_map/dot_general | solution.py:38
  368.8 1.6 dynamic-slice_bitcast_fusion
  370.4 124.6 %all-reduce.5.cloned.1.call-done = bf16[12288,128]{1,0:T(8,128)(2,1)} async-done(((bf16[12288,128]{1,0:T(8,128)(2,1)}), bf16[12288,128]{1,0:T(8,128)(2,1)}) %all-reduce.5.cloned.1.call-update) | async-done | bytes 3145744 | tf_op jit(solution)/shard_map/psum | solution.py:64
  495.0 1.6 fusion.16
  (4 shorter events, 0.1 us)
Async XLA Ops:
  7.2 184.1 %copy-start = (bf16[1,128,12288]{2,1,0:T(8,128)(2,1)S(1)}, bf16[1,128,12288]{2,1,0:T(8,128)(2,1)}, u32[]{:S(2)}) copy-start(bf16[1,128,12288]{2,1,0:T(8,128)(2,1)} %param.7) | copy-start | bytes 9437188
  7.2 42.6 %all-gather.4.cloned.1.call-start = ((), (), s32[]{:S(2)}) async-start(), calls=%async_computation | async-start | bytes 1671168 | tf_op jit(solution)/shard_map/all_gather | solution.py:27
  7.9 131.6 %all-gather.6.cloned.1.call-start = ((), (), s32[]{:S(2)}) async-start(), calls=%async_computation.1 | async-start | bytes 1671168 | tf_op jit(solution)/shard_map/all_gather | solution.py:41
  8.7 179.0 %all-gather.8.cloned.1.call-start = ((), (), s32[]{:S(2)}) async-start(), calls=%async_computation.2 | async-start | bytes 3342336 | tf_op jit(solution)/shard_map/all_gather | solution.py:28
  9.4 315.5 %all-reduce.3.cloned.1.call-start = ((), (), s32[]{:S(2)}) async-start(), calls=%async_computation.3 | async-start | bytes 6291456 | tf_op jit(solution)/shard_map/psum | solution.py:53
  77.2 62.4 %collective-permute-start.1 = (bf16[12288,64]{0,1:T(8,128)(2,1)}, bf16[12288,64]{0,1:T(8,128)(2,1)}, u32[]{:S(2)}, u32[]{:S(2)}) collective-permute-start(bf16[12288,64]{0,1:T(8,128)(2,1)} %convolution_convert_fusion.4), channel_id=1, source_target_pairs={{16,0},{32,16},{48,32},{64,48},{80,64},{96,80},{112,96},{128,112},... | collective-permute-start | bytes 4718600 | tf_op jit(solution)/shard_map/ppermute | solution.py:10
  78.5 112.9 %copy-start.3 = (bf16[128,64]{0,1:T(8,128)(2,1)S(1)}, bf16[128,64]{0,1:T(8,128)(2,1)}, u32[]{:S(2)}) copy-start(bf16[128,64]{0,1:T(8,128)(2,1)} %param.12) | copy-start | bytes 49156
  78.5 112.8 %collective-permute-start = (bf16[128,64]{0,1:T(8,128)(2,1)S(1)}, bf16[128,64]{0,1:T(8,128)(2,1)S(1)}, u32[]{:S(2)}, u32[]{:S(2)}) collective-permute-start(bf16[128,64]{0,1:T(8,128)(2,1)S(1)} %convolution_convert_fusion.6), channel_id=1, source_target_pairs={{16,0},{32,16},{48,32},{64,48},{80,64},{96,80},{112,96},{128,112},... | collective-permute-start | bytes 49160 | tf_op jit(solution)/shard_map/ppermute | solution.py:10
  194.3 300.7 %all-reduce.5.cloned.1.call-start = ((), (), s32[]{:S(2)}) async-start(), calls=%async_computation.4 | async-start | bytes 6291456 | tf_op jit(solution)/shard_map/psum | solution.py:64
  355.9 1.6 copy-start.1
  355.9 2.5 copy-start.2
Sparse Core Ops, SparseCore 0:
  9.8 39.8 all-gather.3
  52.4 87.1 all-gather.5
  141.4 46.2 all-gather.7
  194.4 130.3 all-reduce.2
  362.8 132.2 all-reduce.4
where the time goes:
time: 503 us
  waiting for transfers between devices  405 us (81%)
  matrix products  41.4 us (8%)
  other arithmetic  36.6 us (7%)
  between operations  14 us (3%)
    psum x1, waiting for transfers between devices, body(): lax.psum(partial_value.astype(jnp.bfloat16), 'dp').astype(jnp.float32)  130 us
    psum x1, waiting for transfers between devices, body(): total = lax.psum(term.astype(jnp.bfloat16), 'dp').astype(jnp.float32)  125 us
    all_gather x1, waiting for transfers between devices, body(): beyond = lax.all_gather(outside_right, 'section', axis=1, tiled=True)[0]  59.8 us
    all_gather x1, waiting for transfers between devices, body(): lax.all_gather(weight_basis, 'dp', axis=1, tiled=True)  48.2 us
    all_gather x1, waiting for transfers between devices, body(): lax.all_gather(act_basis, 'dp', axis=1, tiled=True)  40.3 us
    another operation x6, other arithmetic, orthonormal(): factor = jnp.linalg.cholesky(gram)  18.9 us
    another operation x4, other arithmetic, orthonormal(): return jax.scipy.linalg.solve_triangular(factor, block.T, lower=True).T  16 us
  transfers between devices with their start and end apart: 7, of which 5 were waited for; matrix products, arithmetic and copies ran while one was open for 8% of the time, Pallas kernels for 0%

commit v1 on v0

v1 whole, which is shorter than its diff:
```python
import functools

import jax
import jax.numpy as jnp
from jax import lax
from jax.experimental import pallas as pl
from jax.experimental.pallas import tpu as pltpu
from jax.sharding import PartitionSpec as P

BF = jnp.bfloat16
F32 = jnp.float32
HIGHEST = lax.Precision.HIGHEST
VMEM_LIMIT = 48 * 1024 * 1024
PARAMS = pltpu.CompilerParams(vmem_limit_bytes=VMEM_LIMIT)
NN = (((1,), (0,)), ((), ()))
NT = (((1,), (1,)), ((), ()))
TN = (((0,), (0,)), ((), ()))


def dot(a, b, dims=NN, precision=None):
    return lax.dot_general(a, b, dims, precision=precision, preferred_element_type=F32)


def inverse_factor(gram):
    n = gram.shape[0]
    lane = lax.broadcasted_iota(jnp.int32, (1, n), 1)
    lane8 = lax.broadcasted_iota(jnp.int32, (8, n), 1)
    sub = lax.broadcasted_iota(jnp.int32, (8, n), 0)
    sub1 = lax.broadcasted_iota(jnp.int32, (8, 1), 0)
    work = gram
    done = []
    for first in range(0, n, 8):
        top = work[:8]
        rest = work[8:] if first + 8 < n else None
        for r in range(8):
            k = first + r
            pivot = top[r : r + 1, k : k + 1]
            scale = lax.rsqrt(pivot)
            scale = scale * (1.5 - 0.5 * pivot * scale * scale)
            row = jnp.where(lane == k, scale, top[r : r + 1, :] * scale)
            column = jnp.where(sub1 > r, top[:, k : k + 1] * scale, 0.0)
            cleared = jnp.where((lane8 == k) & (sub > r), 0.0, top)
            top = jnp.where(sub == r, row, cleared - column * row)
            if rest is not None:
                rest = jnp.where(lane == k, 0.0, rest) - (rest[:, k : k + 1] * scale) * row
        done.append(top)
        work = rest
    full = jnp.concatenate(done, axis=0)
    rows = lax.broadcasted_iota(jnp.int32, (n, n), 0)
    columns = lax.broadcasted_iota(jnp.int32, (n, n), 1)
    return jnp.where(columns <= rows, full, 0.0)


def proj_kernel(me_ref, g_ref, e_ref, own_ref, other_ref, left_ref, left_t_ref, acc):
    step = pl.program_id(0)
    width = own_ref.shape[1]
    core = lax.rem(me_ref[0], 2)
    mine = pl.ds(pl.multiple_of(core * width, width), width)
    others = pl.ds(pl.multiple_of((1 - core) * width, width), width)
    own, other = own_ref[...], other_ref[...]
    term = dot(g_ref[:, mine], own, NT) + dot(e_ref[:, mine], own, NT)
    term += dot(g_ref[:, others], other, NT) + dot(e_ref[:, others], other, NT)

    @pl.when(step == 0)
    def _():
        acc[...] = term

    @pl.when(step > 0)
    def _():
        acc[...] += term

    @pl.when(step == pl.num_programs(0) - 1)
    def _():
        proj = acc[...]
        inverse = inverse_factor(dot(proj, proj, TN, HIGHEST))
        left = dot(proj, inverse, NT, HIGHEST)
        left_ref[...] = left.astype(BF)
        left_t_ref[...] = left.T.astype(BF)


def act_left(me, grad, error, own, other):
    _, rows, width = grad.shape
    pieces, rank, part = own.shape
    pair = width // pieces
    wide = pl.BlockSpec((None, rows, pair), lambda m, me: (0, 0, (me[0] // 2) ^ m))
    narrow = pl.BlockSpec((None, rank, part), lambda m, me: (m, 0, 0))
    return pl.pallas_call(
        proj_kernel,
        grid_spec=pltpu.PrefetchScalarGridSpec(
            num_scalar_prefetch=1,
            grid=(pieces,),
            in_specs=[wide, wide, narrow, narrow],
            out_specs=[
                pl.BlockSpec((rows, rank), lambda m, me: (0, 0)),
                pl.BlockSpec((rank, rows), lambda m, me: (0, 0)),
            ],
            scratch_shapes=[pltpu.VMEM((rows, rank), F32)],
        ),
        out_shape=[jax.ShapeDtypeStruct((rows, rank), BF), jax.ShapeDtypeStruct((rank, rows), BF)],
        compiler_params=PARAMS,
    )(me, grad, error, own, other)


def right_kernel(g_ref, e_ref, left_ref, left_t_ref, error_ref, right_ref):
    g, e = g_ref[...], e_ref[...]
    left_t = left_t_ref[...]
    right = (dot(left_t, g) + dot(left_t, e)).astype(BF)
    rebuilt = dot(left_ref[...], right)
    error_ref[...] = (g.astype(F32) + e.astype(F32) - rebuilt).astype(BF)
    part = right_ref.shape[2]
    for i in range(right_ref.shape[0]):
        right_ref[i] = right[:, i * part : (i + 1) * part]


def act_right(grad, error, left, left_t, parts):
    _, rows, width = grad.shape
    rank = left_t.shape[0]
    steps = parts // 2
    wide = pl.BlockSpec((None, rows, width // steps), lambda m: (0, 0, m))
    return pl.pallas_call(
        right_kernel,
        grid=(steps,),
        in_specs=[
            wide,
            wide,
            pl.BlockSpec((rows, rank), lambda m: (0, 0)),
            pl.BlockSpec((rank, rows), lambda m: (0, 0)),
        ],
        out_specs=[wide, pl.BlockSpec((2, rank, width // parts), lambda m: (m, 0, 0))],
        out_shape=[
            jax.ShapeDtypeStruct(grad.shape, BF),
            jax.ShapeDtypeStruct((parts, rank, width // parts), BF),
        ],
        compiler_params=PARAMS,
    )(grad, error, left, left_t)


def inner_kernel(right_ref, basis_ref, *refs):
    outside, (inner_ref, used_ref) = refs[:-2], refs[-2:]
    group = outside[0].shape[0]

    def total(piece):
        acc = None
        for i in range(right_ref.shape[0]):
            right = piece(i)
            used_ref[i] = right
            term = dot(right, basis_ref[i])
            acc = term if acc is None else acc + term
        inner_ref[...] = acc.astype(BF)

    first = lax.axis_index("section") == 0

    @pl.when(first)
    def _():
        total(lambda i: outside[i // group][i % group])

    @pl.when(jnp.logical_not(first))
    def _():
        total(lambda i: right_ref[i])


def inner_of(right, basis, outside):
    return pl.pallas_call(
        inner_kernel,
        out_shape=[
            jax.ShapeDtypeStruct((right.shape[1], basis.shape[2]), BF),
            jax.ShapeDtypeStruct(right.shape, BF),
        ],
        compiler_params=PARAMS,
    )(right, basis, *outside)


def core_kernel(x_ref, left_t_ref, outside_ref, out_ref):
    last = lax.axis_index("section") == lax.axis_size("section") - 1
    left_t = jnp.where(last, outside_ref[...].astype(F32), left_t_ref[...].astype(F32)).astype(BF)
    core = dot(left_t, x_ref[...]).astype(BF)
    count, _, part = out_ref.shape
    for i in range(count):
        out_ref[i] = core[:, i * part : (i + 1) * part]


def core_of(inputs, left_t, outside_left_t, parts):
    _, rows, width = inputs.shape
    rank = left_t.shape[0]
    steps = parts // 2
    small = pl.BlockSpec((rank, rows), lambda m: (0, 0))
    return pl.pallas_call(
        core_kernel,
        grid=(steps,),
        in_specs=[pl.BlockSpec((None, rows, width // steps), lambda m: (0, 0, m)), small, small],
        out_specs=pl.BlockSpec((2, rank, width // parts), lambda m: (m, 0, 0)),
        out_shape=jax.ShapeDtypeStruct((parts, rank, width // parts), BF),
        compiler_params=PARAMS,
    )(inputs, left_t, outside_left_t)


def three_parts(value):
    high = value.astype(BF).astype(F32)
    value = value - high
    middle = value.astype(BF).astype(F32)
    return high, middle, (value - middle).astype(BF).astype(F32)


def sum_kernel(cores_ref, inner_ref, left_sum_ref, message_ref):
    count, rank, part = cores_ref.shape
    cores_t = cores_ref[...].reshape(count * rank, part)
    inner = inner_ref[...].reshape(count * rank, -1)
    left_sum = dot(inner, cores_t, TN)
    left_sum_ref[...] = left_sum
    high = left_sum.astype(BF)
    low = (left_sum - high.astype(F32)).astype(BF)
    mid = (dot(cores_t, high, NT) + dot(cores_t, low, NT)).astype(BF)
    gram = dot(left_sum, left_sum, NT, HIGHEST)
    share = gram.shape[0] // count
    for i in range(count):
        high, middle, low = three_parts(gram[i * share : (i + 1) * share])
        message_ref[i, :rank] = mid[i * rank : (i + 1) * rank]
        message_ref[i, rank : rank + 16] = jnp.concatenate([high, middle]).astype(BF)
        message_ref[i, rank + 16 :] = jnp.concatenate([low, jnp.zeros_like(low)]).astype(BF)


def local_sum(cores, inner):
    count, rank, part = cores.shape
    extra = inner.shape[2]
    return pl.pallas_call(
        sum_kernel,
        out_shape=[
            jax.ShapeDtypeStruct((extra, part), F32),
            jax.ShapeDtypeStruct((count, rank + 32, extra), BF),
        ],
        compiler_params=PARAMS,
    )(cores, inner)


def reduce_kernel(received_ref, mid_ref, gram_ref):
    count, rows, _ = received_ref.shape
    rank = rows - 32
    total = received_ref[0].astype(F32)
    for i in range(1, count):
        total += received_ref[i].astype(F32)
    mid_ref[...] = total[:rank].astype(BF)
    gram = total[rank : rank + 8] + total[rank + 8 : rank + 16] + total[rank + 16 : rank + 24]
    for i in range(count):
        gram_ref[i] = gram


def reduced(received):
    count, rows, extra = received.shape
    return pl.pallas_call(
        reduce_kernel,
        out_shape=[
            jax.ShapeDtypeStruct((rows - 32, extra), BF),
            jax.ShapeDtypeStruct((count, extra // count, extra), F32),
        ],
        compiler_params=PARAMS,
    )(received)


def left_kernel(left_sum_ref, gram_ref, left_ref, inverse_ref):
    extra = left_sum_ref.shape[0]
    inverse = inverse_factor(gram_ref[...].reshape(extra, extra))
    inverse_ref[...] = inverse
    left = lax.dot_general(
        left_sum_ref[...],
        inverse,
        (((0,), (1,)), ((), ())),
        precision=HIGHEST,
        preferred_element_type=F32,
    )
    left_ref[...] = left.astype(BF)


def weight_left_of(left_sum, gram):
    extra, part = left_sum.shape
    return pl.pallas_call(
        left_kernel,
        out_shape=[
            jax.ShapeDtypeStruct((part, extra), BF),
            jax.ShapeDtypeStruct((extra, extra), F32),
        ],
        compiler_params=PARAMS,
    )(left_sum, gram)


def product_kernel(right_ref, mids_ref, out_ref):
    count, rank, part = right_ref.shape
    right = right_ref[...].reshape(count * rank, part)
    out_ref[...] = dot(right, mids_ref[...].reshape(count * rank, -1), TN).astype(out_ref.dtype)


def product_of(rights, mids):
    return pl.pallas_call(
        product_kernel,
        out_shape=jax.ShapeDtypeStruct((rights.shape[2], mids.shape[2]), F32),
        compiler_params=PARAMS,
    )(rights, mids)


def scale_kernel(product_ref, inverse_ref, out_ref):
    out_ref[...] = dot(product_ref[...], inverse_ref[...], NT, HIGHEST).astype(BF)


def weight_right_of(product, inverse):
    return pl.pallas_call(
        scale_kernel,
        out_shape=jax.ShapeDtypeStruct(product.shape, BF),
        compiler_params=PARAMS,
    )(product, inverse)


def gather_by_chip(value):
    size = lax.axis_size("dp")
    pieces = [value]
    for m in range(1, size // 2):
        pieces.append(lax.ppermute(value, "dp", [(d, d ^ (2 * m)) for d in range(size)]))
    own = jnp.stack(pieces)
    return own, lax.ppermute(own, "dp", [(d, d ^ 1) for d in range(size)])


def gather_to_first(value):
    size = lax.axis_size("section")
    step = size // 4
    pieces = [value]
    for t in range(1, step):
        pieces.append(
            lax.ppermute(value, "section", [(s + t, s) for s in range(0, size, step)])
        )
    group = jnp.stack(pieces)
    groups = [group]
    for u in range(1, 4):
        groups.append(lax.ppermute(group, "section", [(u * step, 0)]))
    return groups


def spread(value):
    copies = jnp.broadcast_to(value[None], (lax.axis_size("dp"),) + value.shape)
    return lax.all_to_all(copies, "dp", 0, 0)


def after(value, *others):
    return lax.optimization_barrier((value, *others))[0]


def body(
    section_input, boundary_grad, carry_error, act_basis, weight_basis, outside_left, outside_right
):
    sections, parts = lax.axis_size("section"), lax.axis_size("dp")
    down = [(s, (s - 1) % sections) for s in range(sections)]
    up = [(s, (s + 1) % sections) for s in range(sections)]
    me = lax.axis_index("dp").astype(jnp.int32).reshape(1)

    basis_w = lax.ppermute(weight_basis[0], "section", up)
    own, other = gather_by_chip(act_basis[0].T)
    basis_w = lax.all_gather(basis_w, "dp", axis=0)
    groups = gather_to_first(outside_right[0].T)

    left, left_t = act_left(me, boundary_grad, carry_error, after(own, groups[0]), other)
    recv_left = lax.ppermute(left_t, "section", down)
    new_error, right = act_right(boundary_grad, carry_error, left, left_t, parts)
    cores = core_of(section_input, recv_left, outside_left.T, parts)
    cores = lax.all_to_all(cores, "dp", 0, 0)

    inner, rights = inner_of(right, basis_w, groups)
    inner = spread(lax.ppermute(inner, "section", down))
    rights = lax.all_to_all(after(rights, cores, inner), "dp", 0, 0)

    left_sum, message = local_sum(cores, inner)
    mid, gram = reduced(lax.all_to_all(message, "dp", 0, 0))
    gram = lax.all_to_all(gram, "dp", 0, 0)
    mids = spread(lax.ppermute(mid, "section", up))
    weight_left, inverse = weight_left_of(left_sum, gram)
    product = lax.ppermute(product_of(rights, mids), "section", down)
    weight_right = weight_right_of(product, inverse)
    return (new_error, weight_left[None], weight_right[None])


def solution(mesh):
    return jax.shard_map(
        body,
        mesh=mesh,
        in_specs=(
            P("section", "dp", None),
            P("section", "dp", None),
            P("section", "dp", None),
            P("section", "dp", None),
            P("section", "dp", None),
            P("dp", None),
            P("dp", "section", None),
        ),
        out_specs=(P("section", "dp", None), P("section", "dp", None), P("section", "dp", None)),
        check_vma=False,
    )
```

time: 503 us -> 236 us (0.47)
  waiting for transfers between devices: 405 us -> 58.5 us
  blocking collectives: 0 us -> 66 us
  Pallas kernels: 0 us -> 42.6 us
  matrix products: 41.4 us -> 0 us
  other arithmetic: 36.6 us -> 0.95 us
  starting transfers between devices: 2.95 us -> 37.9 us
  local copies, waits for them, and re-layouts: 3.04 us -> 14.8 us
    psum x2 -> x0, waiting for transfers between devices: 255 us -> none  [the longest x1 130 us: body(): lax.psum(partial_value.astype(jnp.bfloat16), 'dp').astype(jnp.float32)]
    all_gather x3 -> x1, waiting for transfers between devices: 148 us -> 0.01 us  [body(): basis_w = lax.all_gather(basis_w, 'dp', axis=0)]
    all_to_all x0 -> x4, blocking collectives: none -> 66 us  [the longest x1 24.5 us: body(): rights = lax.all_to_all(after(rights, cores, inner), 'dp', 0, 0)]
    ppermute x2 -> x19, waiting for transfers between devices: 0.01 us -> 51.3 us  [the longest x3 10.4 us: gather_to_first(): groups.append(lax.ppermute(group, 'section', [(u * step, 0)]))]
    pallas_call x0 -> x9, Pallas kernels: none -> 42.6 us  [the longest x1 12.9 us: weight_left_of(): pl.pallas_call(left_kernel, out_shape=[jax.ShapeDtypeStruct((part, extra)...]
    dot_general x10 -> x0, matrix products: 36.9 us -> none  [the longest x1 7.41 us: body(): jnp.dot(merged, basis_a.astype(jnp.float32), precision=lax.Precision.HIGH...]
    another operation x10 -> x1, other arithmetic: 34.9 us -> 0.95 us  [gather_to_first(): group = jnp.stack(pieces)]
    ppermute x2 -> x19, starting transfers between devices: 2.57 us -> 26.2 us  [the longest x7 10.1 us: gather_by_chip(): lax.ppermute(value, 'dp', [(d, d ^ 2 * m) for d in range(size)])]
  transfers between devices with their start and end apart: 7 -> 22, of which waited for: 5 -> 10; matrix products, arithmetic and copies ran while one was open for 8% -> 1% of each run, Pallas kernels for 0% -> 16%
where the time goes in v1:
time: 236 us; the launch traced here: 235 us
  blocking collectives  66 us (28%)
  waiting for transfers between devices  58.5 us (25%)
  Pallas kernels  42.6 us (18%)
  starting transfers between devices  37.9 us (16%)
  local copies, waits for them, and re-layouts  14.8 us (6%)
  between operations  14.3 us (6%)
    all_to_all x1, blocking collectives, body(): rights = lax.all_to_all(after(rights, cores, inner), 'dp', 0, 0)  24.5 us
    all_to_all x1, blocking collectives, body(): gram = lax.all_to_all(gram, 'dp', 0, 0)  15.1 us
    all_to_all x1, blocking collectives, spread(): return lax.all_to_all(copies, 'dp', 0, 0)  14.5 us
    unnamed x39, local copies, waits for them, and re-layouts  14 us
    pallas_call x1, Pallas kernels, weight_left_of(): pl.pallas_call(left_kernel, out_shape=[jax.ShapeDtypeStruct((part, extra)...  12.9 us
    pallas_call x1, Pallas kernels, act_left(): pl.pallas_call(proj_kernel, grid_spec=pltpu.PrefetchScalarGridSpec(num_sc...  12.6 us
    all_to_all x1, blocking collectives, body(): mid, gram = reduced(lax.all_to_all(message, 'dp', 0, 0))  11.9 us
    ppermute x3, waiting for transfers between devices, gather_to_first(): groups.append(lax.ppermute(group, 'section', [(u * step, 0)]))  10.4 us
  transfers between devices with their start and end apart: 22, of which 10 were waited for; matrix products, arithmetic and copies ran while one was open for 1% of the time, Pallas kernels for 16%

profile of v1, /device:TPU:1, one launch (start us, length us, event | category | flops | bytes accessed | tf_op | source)
XLA Modules:
  0.0 235.0 jit_solution(1574298523845614121)
XLA Ops:
  7.2 0.0 all-gather.3.cloned.1.call-start
  7.2 3.7 %collective-permute-start.12 = (bf16[768,128]{1,0:T(8,128)(2,1)}, bf16[768,128]{1,0:T(8,128)(2,1)S(1)}, u32[]{:S(2)}, u32[]{:S(2)}) collective-permute-start(bf16[768,128]{1,0:T(8,128)(2,1)} %bitcast.51), channel_id=1, source_target_pairs={{0,16},{16,32},{32,48},{48,64},{64,80},{80,96},{96,112},{112,128},... | collective-permute-start | bytes 589832 | tf_op jit(solution)/shard_map/ppermute | solution.py:352
  10.9 10.1 %collective-permute-done.12 = bf16[768,128]{1,0:T(8,128)(2,1)S(1)} collective-permute-done((bf16[768,128]{1,0:T(8,128)(2,1)}, bf16[768,128]{1,0:T(8,128)(2,1)S(1)}, u32[]{:S(2)}, u32[]{:S(2)}) %collective-permute-start.12) | collective-permute-done | bytes 196640 | tf_op jit(solution)/shard_map/ppermute | solution.py:352
  21.0 0.7 copy-done.15
  21.7 0.0 all-gather.3.cloned.1.call-update
  21.7 1.4 collective-permute-start
  23.1 2.6 %collective-permute-start.1 = (bf16[64,768]{1,0:T(8,128)(2,1)}, bf16[64,768]{1,0:T(8,128)(2,1)S(1)}, u32[]{:S(2)}, u32[]{:S(2)}) collective-permute-start(bf16[64,768]{1,0:T(8,128)(2,1)} %bitcast.45), channel_id=1, source_target_pairs={{0,4},{1,5},{2,6},{3,7},{4,0},{5,1},{6,2},{7,3},{8,12},{9,13},{10,... | collective-permute-start | bytes 294920 | tf_op jit(solution)/shard_map/ppermute | solution.py:315
  25.7 0.0 collective-permute-start.2
  25.7 0.3 collective-permute-start.3
  26.0 0.9 collective-permute-start.4
  26.9 0.9 bitcast_dynamic-update-slice_fusion
  27.8 3.9 %collective-permute-start.5 = (bf16[64,768]{1,0:T(8,128)(2,1)}, bf16[64,768]{1,0:T(8,128)(2,1)S(1)}, u32[]{:S(2)}, u32[]{:S(2)}) collective-permute-start(bf16[64,768]{1,0:T(8,128)(2,1)} %bitcast.49), channel_id=1, source_target_pairs={{0,12},{1,13},{2,14},{3,15},{4,8},{5,9},{6,10},{7,11},{8,4},{9,5},... | collective-permute-start | bytes 294920 | tf_op jit(solution)/shard_map/ppermute | solution.py:315
  31.8 1.0 collective-permute-start.6
  32.9 2.5 %collective-permute-done.5 = bf16[64,768]{1,0:T(8,128)(2,1)S(1)} collective-permute-done((bf16[64,768]{1,0:T(8,128)(2,1)}, bf16[64,768]{1,0:T(8,128)(2,1)S(1)}, u32[]{:S(2)}, u32[]{:S(2)}) %collective-permute-start.5) | collective-permute-done | bytes 98336 | tf_op jit(solution)/shard_map/ppermute | solution.py:315
  35.4 5.4 %collective-permute-done.6 = bf16[64,768]{1,0:T(8,128)(2,1)S(1)} collective-permute-done((bf16[64,768]{1,0:T(8,128)(2,1)}, bf16[64,768]{1,0:T(8,128)(2,1)S(1)}, u32[]{:S(2)}, u32[]{:S(2)}) %collective-permute-start.6) | collective-permute-done | bytes 98336 | tf_op jit(solution)/shard_map/ppermute | solution.py:315
  40.8 3.7 %collective-permute-start.10 = (bf16[8,64,768]{2,1,0:T(8,128)(2,1)S(1)}, bf16[8,64,768]{2,1,0:T(8,128)(2,1)S(1)}, u32[]{:S(2)}, u32[]{:S(2)}) collective-permute-start(bf16[8,64,768]{2,1,0:T(8,128)(2,1)S(1)} %bitcast_dynamic-update-slice_fusion.1.own_ref), channel_id=1, source_target_pairs={{0,1},{1,0},{2,3},{3,2},{4,5},{5,4},{6,7},{7,6},{8,9},{9,8},{10,11... | collective-permute-start | bytes 2359304 | tf_op jit(solution)/shard_map/ppermute | solution.py:317
  44.5 1.3 collective-permute-start.7
  45.8 1.3 collective-permute-start.8
  47.1 1.3 collective-permute-start.9
  48.4 8.4 %collective-permute-done.7 = bf16[64,768]{1,0:T(8,128)(2,1)S(1)} collective-permute-done((bf16[64,768]{1,0:T(8,128)(2,1)}, bf16[64,768]{1,0:T(8,128)(2,1)S(1)}, u32[]{:S(2)}, u32[]{:S(2)}) %collective-permute-start.7) | collective-permute-done | bytes 98336 | tf_op jit(solution)/shard_map/ppermute | solution.py:326
  56.9 0.9 pad_maximum_fusion.refs_0_
  57.8 0.0 copy-start
  57.8 1.9 copy-done
  59.7 12.6 %shard_map.94 = (bf16[128,64]{1,0:T(8,128)(2,1)S(1)}, bf16[64,128]{1,0:T(8,128)(2,1)S(1)}) custom-call(s32[1]{0:T(128)} %bitcast.me_ref, bf16[1,128,12288]{2,1,0:T(8,128)(2,1)S(1)} %copy-done, bf16[1,128,12288]{2,1,0:T(8,128)(2,1)} %e_ref.3, bf16[8,64,768]{2,1,0:T(8,128)(2,1)S(1)} %bitcast_dynamic-update-slice_fusion.1.own_ref, ...), custom_call_target="tpu_custom_call" | custom-call | tf_op jit(solution)/shard_map/pallas_call | solution.py:87
  72.4 0.0 copy-start.12
  72.4 0.6 copy-done.12
  73.0 4.1 %collective-permute-done.11.left_t_ref = bf16[64,128]{1,0:T(8,128)(2,1)S(1)} collective-permute-done((bf16[64,128]{1,0:T(8,128)(2,1)S(1)}, bf16[64,128]{1,0:T(8,128)(2,1)S(1)}, u32[]{:S(2)}, u32[]{:S(2)}) %collective-permute-start.11) | collective-permute-done | bytes 16416 | tf_op jit(solution)/shard_map/ppermute | solution.py:358
  77.1 1.9 shard_map.96
  79.0 1.2 copy-done.2
  80.2 6.0 %all-to-all-start = ((bf16[16,64,768]{2,1,0:T(8,128)(2,1)}), bf16[16,64,768]{2,1,0:T(8,128)(2,1)}, u32[]{:S(2)}, u32[]{:S(2)}) async-start(bf16[16,64,768]{2,1,0:T(8,128)(2,1)} %copy-done.2), calls=%async_computation | async-start | bytes 3145728 | tf_op jit(solution)/shard_map/all_to_all | solution.py:361
  86.2 1.3 collective-permute-start.13
  87.5 1.3 collective-permute-start.14
  88.8 1.3 collective-permute-start.15
  90.1 0.0 copy-start.13
  90.1 0.7 copy-done.13
  90.9 7.8 %shard_map.95 = (bf16[1,128,12288]{2,1,0:T(8,128)(2,1)}, bf16[16,64,768]{2,1,0:T(8,128)(2,1)S(1)}) custom-call(bf16[1,128,12288]{2,1,0:T(8,128)(2,1)S(1)} %copy-done.1, bf16[1,128,12288]{2,1,0:T(8,128)(2,1)} %e_ref.3, bf16[128,64]{1,0:T(8,128)(2,1)S(1)} %copy-done.13, bf16[64,128]{1,0:T(8,128)(2,1)S(1)} %get-tuple-element.19.left_t_ref), custom_call_target="tpu_custom_call" | custom-call | tf_op jit(solution)/shard_map/pallas_call | solution.py:120
  98.6 1.2 copy-done.4
  99.8 0.8 copy-done.6
  100.6 3.1 %collective-permute-done.14.refs_2_ = bf16[4,64,768]{2,1,0:T(8,128)(2,1)S(1)} collective-permute-done((bf16[4,64,768]{2,1,0:T(8,128)(2,1)S(1)}, bf16[4,64,768]{2,1,0:T(8,128)(2,1)S(1)}, u32[]{:S(2)}, u32[]{:S(2)}) %collective-permute-start.14) | collective-permute-done | bytes 393248 | tf_op jit(solution)/shard_map/ppermute | solution.py:331
  103.7 0.8 copy-done.8
  104.5 7.3 %collective-permute-done.15.refs_3_ = bf16[4,64,768]{2,1,0:T(8,128)(2,1)S(1)} collective-permute-done((bf16[4,64,768]{2,1,0:T(8,128)(2,1)S(1)}, bf16[4,64,768]{2,1,0:T(8,128)(2,1)S(1)}, u32[]{:S(2)}, u32[]{:S(2)}) %collective-permute-start.15) | collective-permute-done | bytes 393248 | tf_op jit(solution)/shard_map/ppermute | solution.py:331
  111.8 0.7 copy-done.10
  112.5 1.4 copy-done.5
  114.0 1.0 copy-done.7
  114.9 1.0 copy-done.9
  115.9 1.0 copy-done.11
  116.9 2.5 %shard_map.97 = (bf16[64,128]{1,0:T(8,128)(2,1)S(1)}, bf16[16,64,768]{2,1,0:T(8,128)(2,1)S(1)}) custom-call(bf16[16,64,768]{2,1,0:T(8,128)(2,1)S(1)} %copy-done.5, bf16[16,768,128]{2,1,0:T(8,128)(2,1)} %bitcast.35, bf16[4,64,768]{2,1,0:T(8,128)(2,1)S(1)} %pad_maximum_fusion.refs_0_, bf16[4,64,768]{2,1,0:T(8,128)(2,1)S(1)} %copy-done.7, ...), custom_call_target="tpu_custom_call" | custom-call | tf_op jit(solution)/shard_map/pallas_call | solution.py:163
  119.5 0.1 collective-permute-start.16
  119.6 4.1 %collective-permute-done.16 = bf16[64,128]{1,0:T(8,128)(2,1)S(1)} collective-permute-done((bf16[64,128]{1,0:T(8,128)(2,1)S(1)}, bf16[64,128]{1,0:T(8,128)(2,1)S(1)}, u32[]{:S(2)}, u32[]{:S(2)}) %collective-permute-start.16) | collective-permute-done | bytes 16416 | tf_op jit(solution)/shard_map/ppermute | solution.py:364
  123.7 14.5 %all_to_all.30.inner_ref = bf16[16,64,128]{2,1,0:T(8,128)(2,1)S(1)} all-to-all(bf16[16,64,128]{2,1,0:T(8,128)(2,1)S(1)} %broadcast_in_dim.8), channel_id=1, replica_groups=mesh['section'=16,'dp'=16] {'dp'}, dimensions={0} | all-to-all | bytes 524288 | tf_op jit(solution)/shard_map/all_to_all | solution.py:337
  138.2 3.1 %shard_map.98 = (f32[128,768]{1,0:T(8,128)S(1)}, bf16[16,96,128]{2,1,0:T(8,128)(2,1)S(1)}) custom-call(bf16[16,64,768]{2,1,0:T(8,128)(2,1)} %all-to-all-done.cores_ref, bf16[16,64,128]{2,1,0:T(8,128)(2,1)S(1)} %all_to_all.30.inner_ref), custom_call_target="tpu_custom_call" | custom-call | tf_op jit(solution)/shard_map/pallas_call | solution.py:225
  141.3 11.9 %all_to_all.31.received_ref = bf16[16,96,128]{2,1,0:T(8,128)(2,1)S(1)} all-to-all(bf16[16,96,128]{2,1,0:T(8,128)(2,1)S(1)} %get-tuple-element.24), channel_id=1, replica_groups=mesh['section'=16,'dp'=16] {'dp'}, dimensions={0} | all-to-all | bytes 786432 | tf_op jit(solution)/shard_map/all_to_all | solution.py:368
  153.2 0.1 shard_map.99
  153.2 0.1 collective-permute-start.17
  153.3 6.1 %collective-permute-done.17 = bf16[64,128]{1,0:T(8,128)(2,1)S(1)} collective-permute-done((bf16[64,128]{1,0:T(8,128)(2,1)S(1)}, bf16[64,128]{1,0:T(8,128)(2,1)S(1)}, u32[]{:S(2)}, u32[]{:S(2)}) %collective-permute-start.17) | collective-permute-done | bytes 16416 | tf_op jit(solution)/shard_map/ppermute | solution.py:370
  159.5 0.8 broadcast_in_dim.20
  160.3 5.6 %all-to-all-start.5 = ((bf16[16,64,128]{2,1,0:T(8,128)(2,1)}), bf16[16,64,128]{2,1,0:T(8,128)(2,1)S(1)}, u32[]{:S(2)}, u32[]{:S(2)}) async-start(bf16[16,64,128]{2,1,0:T(8,128)(2,1)} %broadcast_in_dim.20), calls=%async_computation.5 | async-start | bytes 524288 | tf_op jit(solution)/shard_map/all_to_all | solution.py:337
  165.9 7.2 %all-to-all-done.5.mids_ref = bf16[16,64,128]{2,1,0:T(8,128)(2,1)S(1)} async-done(((bf16[16,64,128]{2,1,0:T(8,128)(2,1)}), bf16[16,64,128]{2,1,0:T(8,128)(2,1)S(1)}, u32[]{:S(2)}, u32[]{:S(2)}) %all-to-all-start.5) | async-done | bytes 262176 | tf_op jit(solution)/shard_map/all_to_all | solution.py:337
  173.1 24.5 %all_to_all.32.right_ref = bf16[16,64,768]{2,1,0:T(8,128)(2,1)S(1)} all-to-all(bf16[16,64,768]{2,1,0:T(8,128)(2,1)S(1)} %get-tuple-element.28), channel_id=1, replica_groups=mesh['section'=16,'dp'=16] {'dp'}, dimensions={0} | all-to-all | bytes 3145728 | tf_op jit(solution)/shard_map/all_to_all | solution.py:365
  197.7 0.6 shard_map.101
  198.3 0.8 collective-permute-start.18
  199.1 15.1 %all_to_all.33.gram_ref = f32[16,8,128]{2,1,0:T(8,128)S(1)} all-to-all(f32[16,8,128]{2,1,0:T(8,128)S(1)} %get-tuple-element.25), channel_id=1, replica_groups=mesh['section'=16,'dp'=16] {'dp'}, dimensions={0} | all-to-all | bytes 131072 | tf_op jit(solution)/shard_map/all_to_all | solution.py:369
  214.1 12.9 %shard_map.100 = (bf16[768,128]{1,0:T(8,128)(2,1)}, f32[128,128]{1,0:T(8,128)S(1)}) custom-call(f32[128,768]{1,0:T(8,128)S(1)} %get-tuple-element.23.left_sum_ref, f32[16,8,128]{2,1,0:T(8,128)S(1)} %all_to_all.33.gram_ref), custom_call_target="tpu_custom_call" | custom-call | tf_op jit(solution)/shard_map/pallas_call | solution.py:275
  227.0 1.2 shard_map.102
  (37 shorter events, 0.2 us)
Async XLA Ops:
  7.2 105.4 %all-gather.3.cloned.1.call-start = ((), (), s32[]{:S(2)}) async-start(), calls=%async_computation.6 | async-start | bytes 3342336 | tf_op jit(solution)/shard_map/all_gather | solution.py:354
  7.2 13.8 %collective-permute-start.12 = (bf16[768,128]{1,0:T(8,128)(2,1)}, bf16[768,128]{1,0:T(8,128)(2,1)S(1)}, u32[]{:S(2)}, u32[]{:S(2)}) collective-permute-start(bf16[768,128]{1,0:T(8,128)(2,1)} %bitcast.51), channel_id=1, source_target_pairs={{0,16},{16,32},{32,48},{48,64},{64,80},{80,96},{96,112},{112,128},... | collective-permute-start | bytes 589832 | tf_op jit(solution)/shard_map/ppermute | solution.py:352
  21.0 0.7 copy-start.15
  21.7 6.2 %collective-permute-start = (bf16[64,768]{1,0:T(8,128)(2,1)}, bf16[64,768]{1,0:T(8,128)(2,1)S(1)}, u32[]{:S(2)}, u32[]{:S(2)}) collective-permute-start(bf16[64,768]{1,0:T(8,128)(2,1)} %bitcast.44), channel_id=1, source_target_pairs={{0,2},{1,3},{2,0},{3,1},{4,6},{5,7},{6,4},{7,5},{8,10},{9,11},{10,... | collective-permute-start | bytes 294920 | tf_op jit(solution)/shard_map/ppermute | solution.py:315
  23.1 8.7 %collective-permute-start.1 = (bf16[64,768]{1,0:T(8,128)(2,1)}, bf16[64,768]{1,0:T(8,128)(2,1)S(1)}, u32[]{:S(2)}, u32[]{:S(2)}) collective-permute-start(bf16[64,768]{1,0:T(8,128)(2,1)} %bitcast.45), channel_id=1, source_target_pairs={{0,4},{1,5},{2,6},{3,7},{4,0},{5,1},{6,2},{7,3},{8,12},{9,13},{10,... | collective-permute-start | bytes 294920 | tf_op jit(solution)/shard_map/ppermute | solution.py:315
  25.7 7.1 %collective-permute-start.2 = (bf16[64,768]{1,0:T(8,128)(2,1)}, bf16[64,768]{1,0:T(8,128)(2,1)S(1)}, u32[]{:S(2)}, u32[]{:S(2)}) collective-permute-start(bf16[64,768]{1,0:T(8,128)(2,1)} %bitcast.46), channel_id=1, source_target_pairs={{0,6},{1,7},{2,4},{3,5},{4,2},{5,3},{6,0},{7,1},{8,14},{9,15},{10,... | collective-permute-start | bytes 294920 | tf_op jit(solution)/shard_map/ppermute | solution.py:315
  25.7 7.1 %collective-permute-start.3 = (bf16[64,768]{1,0:T(8,128)(2,1)}, bf16[64,768]{1,0:T(8,128)(2,1)S(1)}, u32[]{:S(2)}, u32[]{:S(2)}) collective-permute-start(bf16[64,768]{1,0:T(8,128)(2,1)} %bitcast.47), channel_id=1, source_target_pairs={{0,8},{1,9},{2,10},{3,11},{4,12},{5,13},{6,14},{7,15},{8,0},{9,1},... | collective-permute-start | bytes 294920 | tf_op jit(solution)/shard_map/ppermute | solution.py:315
  26.0 6.8 %collective-permute-start.4 = (bf16[64,768]{1,0:T(8,128)(2,1)}, bf16[64,768]{1,0:T(8,128)(2,1)S(1)}, u32[]{:S(2)}, u32[]{:S(2)}) collective-permute-start(bf16[64,768]{1,0:T(8,128)(2,1)} %bitcast.48), channel_id=1, source_target_pairs={{0,10},{1,11},{2,8},{3,9},{4,14},{5,15},{6,12},{7,13},{8,2},{9,3},... | collective-permute-start | bytes 294920 | tf_op jit(solution)/shard_map/ppermute | solution.py:315
  27.8 7.5 %collective-permute-start.5 = (bf16[64,768]{1,0:T(8,128)(2,1)}, bf16[64,768]{1,0:T(8,128)(2,1)S(1)}, u32[]{:S(2)}, u32[]{:S(2)}) collective-permute-start(bf16[64,768]{1,0:T(8,128)(2,1)} %bitcast.49), channel_id=1, source_target_pairs={{0,12},{1,13},{2,14},{3,15},{4,8},{5,9},{6,10},{7,11},{8,4},{9,5},... | collective-permute-start | bytes 294920 | tf_op jit(solution)/shard_map/ppermute | solution.py:315
  31.8 9.0 %collective-permute-start.6 = (bf16[64,768]{1,0:T(8,128)(2,1)}, bf16[64,768]{1,0:T(8,128)(2,1)S(1)}, u32[]{:S(2)}, u32[]{:S(2)}) collective-permute-start(bf16[64,768]{1,0:T(8,128)(2,1)} %bitcast.50), channel_id=1, source_target_pairs={{0,14},{1,15},{2,12},{3,13},{4,10},{5,11},{6,8},{7,9},{8,6},{9,7},... | collective-permute-start | bytes 294920 | tf_op jit(solution)/shard_map/ppermute | solution.py:315
  40.8 17.0 %collective-permute-start.10 = (bf16[8,64,768]{2,1,0:T(8,128)(2,1)S(1)}, bf16[8,64,768]{2,1,0:T(8,128)(2,1)S(1)}, u32[]{:S(2)}, u32[]{:S(2)}) collective-permute-start(bf16[8,64,768]{2,1,0:T(8,128)(2,1)S(1)} %bitcast_dynamic-update-slice_fusion.1.own_ref), channel_id=1, source_target_pairs={{0,1},{1,0},{2,3},{3,2},{4,5},{5,4},{6,7},{7,6},{8,9},{9,8},{10,11... | collective-permute-start | bytes 2359304 | tf_op jit(solution)/shard_map/ppermute | solution.py:317
  44.5 12.3 %collective-permute-start.7 = (bf16[64,768]{1,0:T(8,128)(2,1)}, bf16[64,768]{1,0:T(8,128)(2,1)S(1)}, u32[]{:S(2)}, u32[]{:S(2)}) collective-permute-start(bf16[64,768]{1,0:T(8,128)(2,1)} %bitcast.37), channel_id=1, source_target_pairs={{16,0},{80,64},{144,128},{208,192},{17,1},{81,65},{145,129},{209,1... | collective-permute-start | bytes 294920 | tf_op jit(solution)/shard_map/ppermute | solution.py:326
  45.8 11.1 %collective-permute-start.8 = (bf16[64,768]{1,0:T(8,128)(2,1)}, bf16[64,768]{1,0:T(8,128)(2,1)S(1)}, u32[]{:S(2)}, u32[]{:S(2)}) collective-permute-start(bf16[64,768]{1,0:T(8,128)(2,1)} %bitcast.38), channel_id=1, source_target_pairs={{32,0},{96,64},{160,128},{224,192},{33,1},{97,65},{161,129},{225,1... | collective-permute-start | bytes 294920 | tf_op jit(solution)/shard_map/ppermute | solution.py:326
  47.1 9.8 %collective-permute-start.9 = (bf16[64,768]{1,0:T(8,128)(2,1)}, bf16[64,768]{1,0:T(8,128)(2,1)S(1)}, u32[]{:S(2)}, u32[]{:S(2)}) collective-permute-start(bf16[64,768]{1,0:T(8,128)(2,1)} %bitcast.39), channel_id=1, source_target_pairs={{48,0},{112,64},{176,128},{240,192},{49,1},{113,65},{177,129},{241... | collective-permute-start | bytes 294920 | tf_op jit(solution)/shard_map/ppermute | solution.py:326
  57.8 1.9 copy-start
  59.7 17.4 %copy-start.3 = (bf16[1,128,12288]{2,1,0:T(8,128)(2,1)S(1)}, bf16[1,128,12288]{2,1,0:T(8,128)(2,1)}, u32[]{:S(2)}) copy-start(bf16[1,128,12288]{2,1,0:T(8,128)(2,1)} %x_ref.1) | copy-start | bytes 9437188
  59.7 17.4 %copy-start.14 = (bf16[128,64]{0,1:T(8,128)(2,1)S(1)}, bf16[128,64]{0,1:T(8,128)(2,1)}, u32[]{:S(2)}) copy-start(bf16[128,64]{0,1:T(8,128)(2,1)} %param.12) | copy-start | bytes 49156
  72.4 0.6 copy-start.12
  73.0 4.1 %collective-permute-start.11 = (bf16[64,128]{1,0:T(8,128)(2,1)S(1)}, bf16[64,128]{1,0:T(8,128)(2,1)S(1)}, u32[]{:S(2)}, u32[]{:S(2)}) collective-permute-start(bf16[64,128]{1,0:T(8,128)(2,1)S(1)} %get-tuple-element.19.left_t_ref), channel_id=1, source_target_pairs={{0,240},{16,0},{32,16},{48,32},{64,48},{80,64},{96,80},{112,96},{1... | collective-permute-start | bytes 49160 | tf_op jit(solution)/shard_map/ppermute | solution.py:358
  77.1 13.0 %copy-start.1 = (bf16[1,128,12288]{2,1,0:T(8,128)(2,1)S(1)}, bf16[1,128,12288]{2,1,0:T(8,128)(2,1)}, u32[]{:S(2)}) copy-start(bf16[1,128,12288]{2,1,0:T(8,128)(2,1)} %g_ref.3) | copy-start | bytes 9437188
  79.0 1.2 copy-start.2
  80.2 39.4 %all-to-all-start = ((bf16[16,64,768]{2,1,0:T(8,128)(2,1)}), bf16[16,64,768]{2,1,0:T(8,128)(2,1)}, u32[]{:S(2)}, u32[]{:S(2)}) async-start(bf16[16,64,768]{2,1,0:T(8,128)(2,1)} %copy-done.2), calls=%async_computation | async-start | bytes 3145728 | tf_op jit(solution)/shard_map/all_to_all | solution.py:361
  86.2 13.6 %collective-permute-start.13 = (bf16[4,64,768]{2,1,0:T(8,128)(2,1)S(1)}, bf16[4,64,768]{2,1,0:T(8,128)(2,1)S(1)}, u32[]{:S(2)}, u32[]{:S(2)}) collective-permute-start(bf16[4,64,768]{2,1,0:T(8,128)(2,1)S(1)} %pad_maximum_fusion.refs_0_), channel_id=1, source_target_pairs={{64,0},{65,1},{66,2},{67,3},{68,4},{69,5},{70,6},{71,7},{72,8},{73... | collective-permute-start | bytes 1179656 | tf_op jit(solution)/shard_map/ppermute | solution.py:331
  87.5 16.2 %collective-permute-start.14 = (bf16[4,64,768]{2,1,0:T(8,128)(2,1)S(1)}, bf16[4,64,768]{2,1,0:T(8,128)(2,1)S(1)}, u32[]{:S(2)}, u32[]{:S(2)}) collective-permute-start(bf16[4,64,768]{2,1,0:T(8,128)(2,1)S(1)} %pad_maximum_fusion.refs_0_), channel_id=1, source_target_pairs={{128,0},{129,1},{130,2},{131,3},{132,4},{133,5},{134,6},{135,7},{1... | collective-permute-start | bytes 1179656 | tf_op jit(solution)/shard_map/ppermute | solution.py:331
  88.8 23.0 %collective-permute-start.15 = (bf16[4,64,768]{2,1,0:T(8,128)(2,1)S(1)}, bf16[4,64,768]{2,1,0:T(8,128)(2,1)S(1)}, u32[]{:S(2)}, u32[]{:S(2)}) collective-permute-start(bf16[4,64,768]{2,1,0:T(8,128)(2,1)S(1)} %pad_maximum_fusion.refs_0_), channel_id=1, source_target_pairs={{192,0},{193,1},{194,2},{195,3},{196,4},{197,5},{198,6},{199,7},{2... | collective-permute-start | bytes 1179656 | tf_op jit(solution)/shard_map/ppermute | solution.py:331
  90.1 0.8 copy-start.13
  98.6 1.2 copy-start.4
  99.8 0.8 copy-start.6
  103.7 0.8 copy-start.8
  111.8 0.7 copy-start.10
  112.5 1.4 copy-start.5
  114.0 1.0 copy-start.7
  114.9 1.0 copy-start.9
  115.9 1.0 copy-start.11
  119.5 4.2 %collective-permute-start.16 = (bf16[64,128]{1,0:T(8,128)(2,1)S(1)}, bf16[64,128]{1,0:T(8,128)(2,1)S(1)}, u32[]{:S(2)}, u32[]{:S(2)}) collective-permute-start(bf16[64,128]{1,0:T(8,128)(2,1)S(1)} %get-tuple-element.22), channel_id=1, source_target_pairs={{0,240},{16,0},{32,16},{48,32},{64,48},{80,64},{96,80},{112,96},{1... | collective-permute-start | bytes 49160 | tf_op jit(solution)/shard_map/ppermute | solution.py:364
  153.2 6.3 %collective-permute-start.17 = (bf16[64,128]{1,0:T(8,128)(2,1)S(1)}, bf16[64,128]{1,0:T(8,128)(2,1)S(1)}, u32[]{:S(2)}, u32[]{:S(2)}) collective-permute-start(bf16[64,128]{1,0:T(8,128)(2,1)S(1)} %get-tuple-element.29), channel_id=1, source_target_pairs={{0,16},{16,32},{32,48},{48,64},{64,80},{80,96},{96,112},{112,128},... | collective-permute-start | bytes 49160 | tf_op jit(solution)/shard_map/ppermute | solution.py:370
  160.3 12.9 %all-to-all-start.5 = ((bf16[16,64,128]{2,1,0:T(8,128)(2,1)}), bf16[16,64,128]{2,1,0:T(8,128)(2,1)S(1)}, u32[]{:S(2)}, u32[]{:S(2)}) async-start(bf16[16,64,128]{2,1,0:T(8,128)(2,1)} %broadcast_in_dim.20), calls=%async_computation.5 | async-start | bytes 524288 | tf_op jit(solution)/shard_map/all_to_all | solution.py:337
  198.3 28.7 %collective-permute-start.18 = (f32[768,128]{1,0:T(8,128)S(1)}, f32[768,128]{1,0:T(8,128)S(1)}, u32[]{:S(2)}, u32[]{:S(2)}) collective-permute-start(f32[768,128]{1,0:T(8,128)S(1)} %shard_map.101), channel_id=1, source_target_pairs={{0,240},{16,0},{32,16},{48,32},{64,48},{80,64},{96,80},{112,96},{1... | collective-permute-start | bytes 1179656 | tf_op jit(solution)/shard_map/ppermute | solution.py:372
Sparse Core Ops, SparseCore 0:
  21.8 40.0 all-gather.2

commit v2 on v1

v2 whole, which is shorter than its diff:
```python
import functools

import jax
import jax.numpy as jnp
from jax import lax
from jax.experimental import pallas as pl
from jax.experimental.pallas import tpu as pltpu
from jax.sharding import PartitionSpec as P

BF = jnp.bfloat16
F32 = jnp.float32
HIGHEST = lax.Precision.HIGHEST
VMEM_LIMIT = 20 * 1024 * 1024
PARAMS = pltpu.CompilerParams(vmem_limit_bytes=VMEM_LIMIT)
NN = (((1,), (0,)), ((), ()))
NT = (((1,), (1,)), ((), ()))
TN = (((0,), (0,)), ((), ()))


def dot(a, b, dims=NN, precision=None):
    return lax.dot_general(a, b, dims, precision=precision, preferred_element_type=F32)


def inverse_factor(gram):
    n = gram.shape[0]
    lane = lax.broadcasted_iota(jnp.int32, (8, n), 1)
    sub = lax.broadcasted_iota(jnp.int32, (8, n), 0)
    blocks = [gram[first : first + 8] for first in range(0, n, 8)]
    for b in range(n // 8):
        first = 8 * b
        here = (lane >= first) & (lane < first + 8)

        def spread_columns(block):
            return [jnp.broadcast_to(block[:, k : k + 1], (8, n)) for k in range(first, first + 8)]

        columns = {j: spread_columns(blocks[j]) for j in range(b, n // 8)}
        values = {j: jnp.where(here, 0.0, blocks[j]) for j in columns}
        for r in range(8):
            own = columns[b]
            scale = jnp.broadcast_to(lax.rsqrt(own[r][r : r + 1, :]), (8, n))
            pivot_row = jnp.broadcast_to(values[b][r : r + 1, :], (8, n))
            row = jnp.where(lane == first + r, 1.0, pivot_row) * scale
            scaled = own[r] * scale
            below = jnp.where(sub > r, scaled, 0.0)
            factors = [jnp.broadcast_to(scaled[q : q + 1, :], (8, n)) for q in range(r + 1, 8)]
            for j in columns:
                column = below if j == b else columns[j][r] * scale
                values[j] = values[j] - column * row
                for q in range(r + 1, 8):
                    columns[j][q] = columns[j][q] - column * factors[q - r - 1]
            values[b] = jnp.where(sub == r, row, values[b])
        for j in columns:
            blocks[j] = values[j]
    full = jnp.concatenate(blocks, axis=0)
    rows = lax.broadcasted_iota(jnp.int32, (n, n), 0)
    columns = lax.broadcasted_iota(jnp.int32, (n, n), 1)
    return jnp.where(columns <= rows, full, 0.0)


def columns_of(chip, number, width):
    return pl.ds(pl.multiple_of((chip * 2 + number) * width, width), width)


def first_kernel(g_ref, e_ref, *refs):
    blocks, out_ref = refs[:-1], refs[-1]
    device = lax.axis_index("dp")
    chip, core = device // 2, lax.rem(device, 2)
    proj = None
    for m, block_ref in enumerate(blocks):
        where = columns_of(chip ^ m, core, block_ref.shape[1])
        block = block_ref[...]
        term = dot(g_ref[0, :, where], block, NT) + dot(e_ref[0, :, where], block, NT)
        proj = term if proj is None else proj + term
    out_ref[...] = proj


def first_terms(grad, error, blocks):
    return pl.pallas_call(
        first_kernel,
        out_shape=jax.ShapeDtypeStruct((grad.shape[1], blocks[0].shape[0]), F32),
        compiler_params=PARAMS,
    )(grad, error, *blocks)


def proj_kernel(done, g_ref, e_ref, part_ref, own_ref, other_ref, left_ref, left_t_ref):
    device = lax.axis_index("dp")
    chip, core = device // 2, lax.rem(device, 2)
    pieces, _, width = own_ref.shape
    proj = part_ref[...]
    for block_ref, number, start in ((own_ref, core, done), (other_ref, 1 - core, 0)):
        for m in range(start, pieces):
            where = columns_of(chip ^ m, number, width)
            block = block_ref[m]
            proj += dot(g_ref[0, :, where], block, NT) + dot(e_ref[0, :, where], block, NT)
    inverse = inverse_factor(dot(proj, proj, TN, HIGHEST))
    left = dot(proj, inverse, NT, HIGHEST)
    left_ref[...] = left.astype(BF)
    left_t_ref[...] = left.T.astype(BF)


def act_left(grad, error, part, done, own, other):
    rows, rank = grad.shape[1], own.shape[1]
    return pl.pallas_call(
        functools.partial(proj_kernel, done),
        out_shape=[jax.ShapeDtypeStruct((rows, rank), BF), jax.ShapeDtypeStruct((rank, rows), BF)],
        compiler_params=PARAMS,
    )(grad, error, part, own, other)


def right_kernel(g_ref, e_ref, left_ref, left_t_ref, error_ref, right_ref):
    g, e = g_ref[...], e_ref[...]
    left_t = left_t_ref[...]
    right = (dot(left_t, g) + dot(left_t, e)).astype(BF)
    rebuilt = dot(left_ref[...], right)
    error_ref[...] = (g.astype(F32) + e.astype(F32) - rebuilt).astype(BF)
    part = right_ref.shape[2]
    for i in range(right_ref.shape[0]):
        right_ref[i] = right[:, i * part : (i + 1) * part]


def act_right(grad, error, left, left_t, parts):
    _, rows, width = grad.shape
    rank = left_t.shape[0]
    steps = parts // 2
    wide = pl.BlockSpec((None, rows, width // steps), lambda m: (0, 0, m))
    return pl.pallas_call(
        right_kernel,
        grid=(steps,),
        in_specs=[
            wide,
            wide,
            pl.BlockSpec((rows, rank), lambda m: (0, 0)),
            pl.BlockSpec((rank, rows), lambda m: (0, 0)),
        ],
        out_specs=[wide, pl.BlockSpec((2, rank, width // parts), lambda m: (m, 0, 0))],
        out_shape=[
            jax.ShapeDtypeStruct(grad.shape, BF),
            jax.ShapeDtypeStruct((parts, rank, width // parts), BF),
        ],
        compiler_params=PARAMS,
    )(grad, error, left, left_t)


def core_kernel(x_ref, left_t_ref, outside_ref, out_ref):
    last = lax.axis_index("section") == lax.axis_size("section") - 1
    left_t = jnp.where(last, outside_ref[...].astype(F32), left_t_ref[...].astype(F32)).astype(BF)
    core = dot(left_t, x_ref[...]).astype(BF)
    count, _, part = out_ref.shape
    for i in range(count):
        out_ref[i] = core[:, i * part : (i + 1) * part]


def core_of(inputs, left_t, outside_left_t, parts):
    _, rows, width = inputs.shape
    rank = left_t.shape[0]
    steps = parts // 2
    small = pl.BlockSpec((rank, rows), lambda m: (0, 0))
    return pl.pallas_call(
        core_kernel,
        grid=(steps,),
        in_specs=[pl.BlockSpec((None, rows, width // steps), lambda m: (0, 0, m)), small, small],
        out_specs=pl.BlockSpec((2, rank, width // parts), lambda m: (m, 0, 0)),
        out_shape=jax.ShapeDtypeStruct((parts, rank, width // parts), BF),
        compiler_params=PARAMS,
    )(inputs, left_t, outside_left_t)


def inner_kernel(right_ref, basis_ref, *refs):
    beyond, (inner_ref, message_ref, acc) = refs[:-3], refs[-3:]
    step = pl.program_id(0)
    first = lax.axis_index("section") == 0
    part = right_ref.shape[2]

    @pl.when(step == 0)
    def _():
        acc[...] = jnp.zeros_like(acc)

    def add(blocks_ref):
        term = dot(blocks_ref[0], basis_ref[0])
        for i in range(1, blocks_ref.shape[0]):
            term += dot(blocks_ref[i], basis_ref[i])
        acc[...] += term
        message_ref[:, :, :part] = blocks_ref[...]

    @pl.when(jnp.logical_not(first))
    def _():
        add(right_ref)

    for u, group in enumerate(beyond):

        @pl.when(first & (step == u))
        def _():
            add(group)

    @pl.when(step == pl.num_programs(0) - 1)
    def _():
        inner_ref[...] = acc[...].astype(BF)


def inner_of(right, basis, beyond):
    parts, rank, part = right.shape
    extra = basis.shape[2]
    steps = len(beyond)
    blocks = parts // steps
    return pl.pallas_call(
        inner_kernel,
        grid=(steps,),
        in_specs=[
            pl.BlockSpec((blocks, rank, part), lambda m: (m, 0, 0)),
            pl.BlockSpec((blocks, part, extra), lambda m: (m, 0, 0)),
        ]
        + [pl.BlockSpec(group.shape, lambda m: (0, 0, 0)) for group in beyond],
        out_specs=[
            pl.BlockSpec((rank, extra), lambda m: (0, 0)),
            pl.BlockSpec((blocks, rank, part + extra), lambda m: (m, 0, 0)),
        ],
        out_shape=[
            jax.ShapeDtypeStruct((rank, extra), BF),
            jax.ShapeDtypeStruct((parts, rank, part + extra), BF),
        ],
        scratch_shapes=[pltpu.VMEM((rank, extra), F32)],
        compiler_params=PARAMS,
    )(right, *(pltpu.with_memory_space_constraint(x, pltpu.HBM) for x in (basis, *beyond)))


def place_kernel(inner_ref, _, out_ref, sems):
    parts, _, columns = out_ref.shape
    extra = inner_ref.shape[1]
    copies = [
        pltpu.make_async_copy(
            inner_ref, out_ref.at[i, :, pl.ds(columns - extra, extra)], sems.at[i]
        )
        for i in range(parts)
    ]
    for copy in copies:
        copy.start()
    for copy in copies:
        copy.wait()


def with_inner(message, inner):
    return pl.pallas_call(
        place_kernel,
        in_specs=[pl.BlockSpec(memory_space=pltpu.VMEM), pl.BlockSpec(memory_space=pl.ANY)],
        out_specs=pl.BlockSpec(memory_space=pl.ANY),
        out_shape=jax.ShapeDtypeStruct(message.shape, BF),
        scratch_shapes=[pltpu.SemaphoreType.DMA((message.shape[0],))],
        input_output_aliases={1: 0},
        compiler_params=PARAMS,
    )(inner, message)


def three_parts(value):
    high = value.astype(BF).astype(F32)
    value = value - high
    middle = value.astype(BF).astype(F32)
    return high, middle, (value - middle).astype(BF).astype(F32)


def sum_kernel(cores_ref, inner_ref, left_sum_ref, message_ref):
    count, rank, part = cores_ref.shape
    cores_t = cores_ref[...].reshape(count * rank, part)
    inner = inner_ref[...].reshape(count * rank, -1)
    left_sum = dot(inner, cores_t, TN)
    left_sum_ref[...] = left_sum
    high = left_sum.astype(BF)
    low = (left_sum - high.astype(F32)).astype(BF)
    mid = (dot(cores_t, high, NT) + dot(cores_t, low, NT)).astype(BF)
    gram = dot(left_sum, left_sum, NT, HIGHEST)
    share = gram.shape[0] // count
    for i in range(count):
        high, middle, low = three_parts(gram[i * share : (i + 1) * share])
        message_ref[i, :rank] = mid[i * rank : (i + 1) * rank]
        message_ref[i, rank : rank + 16] = jnp.concatenate([high, middle]).astype(BF)
        message_ref[i, rank + 16 :] = jnp.concatenate([low, jnp.zeros_like(low)]).astype(BF)


def local_sum(cores, received):
    count, rank, part = cores.shape
    extra = received.shape[2] - part
    return pl.pallas_call(
        sum_kernel,
        grid=(1,),
        in_specs=[
            pl.BlockSpec((count, rank, part), lambda i: (0, 0, 0)),
            pl.BlockSpec((count, rank, extra), lambda i: (0, 0, part // extra)),
        ],
        out_specs=[
            pl.BlockSpec((extra, part), lambda i: (0, 0)),
            pl.BlockSpec((count, rank + 32, extra), lambda i: (0, 0, 0)),
        ],
        out_shape=[
            jax.ShapeDtypeStruct((extra, part), F32),
            jax.ShapeDtypeStruct((count, rank + 32, extra), BF),
        ],
        compiler_params=PARAMS,
    )(cores, received)


def reduce_kernel(received_ref, mid_ref, gram_ref):
    count, rows, _ = received_ref.shape
    rank = rows - 32
    total = received_ref[0].astype(F32)
    for i in range(1, count):
        total += received_ref[i].astype(F32)
    mid_ref[...] = total[:rank].astype(BF)
    gram = total[rank : rank + 8] + total[rank + 8 : rank + 16] + total[rank + 16 : rank + 24]
    high, middle, low = three_parts(gram)
    gram_ref[:16] = jnp.concatenate([high, middle]).astype(BF)
    gram_ref[16:] = jnp.concatenate([low, jnp.zeros_like(low)]).astype(BF)


def reduced(received):
    _, rows, extra = received.shape
    return pl.pallas_call(
        reduce_kernel,
        out_shape=[
            jax.ShapeDtypeStruct((rows - 32, extra), BF),
            jax.ShapeDtypeStruct((32, extra), BF),
        ],
        compiler_params=PARAMS,
    )(received)


def copies_kernel(mid_ref, gram_ref, out_ref):
    rank = mid_ref.shape[0]
    for i in range(out_ref.shape[0]):
        out_ref[i, :rank] = mid_ref[...]
        out_ref[i, rank:] = gram_ref[...]


def copies_of(mid, gram, count):
    rows = mid.shape[0] + gram.shape[0]
    return pl.pallas_call(
        copies_kernel,
        out_shape=jax.ShapeDtypeStruct((count, rows, mid.shape[1]), BF),
        compiler_params=PARAMS,
    )(mid, gram)


def left_kernel(left_sum_ref, message_ref, left_ref, inverse_ref):
    count, rows, _ = message_ref.shape
    gram = []
    for i in range(count):
        tail = message_ref[i, rows - 32 :].astype(F32)
        gram.append(tail[:8] + tail[8:16] + tail[16:24])
    inverse = inverse_factor(jnp.concatenate(gram, axis=0))
    inverse_ref[...] = inverse
    left = lax.dot_general(
        left_sum_ref[...],
        inverse,
        (((0,), (1,)), ((), ())),
        precision=HIGHEST,
        preferred_element_type=F32,
    )
    left_ref[...] = left.astype(BF)


def weight_left_of(left_sum, message):
    extra, part = left_sum.shape
    return pl.pallas_call(
        left_kernel,
        out_shape=[
            jax.ShapeDtypeStruct((part, extra), BF),
            jax.ShapeDtypeStruct((extra, extra), F32),
        ],
        compiler_params=PARAMS,
    )(left_sum, message)


def product_kernel(message_ref, right_ref, out_ref):
    count, rank, part = right_ref.shape
    mids = message_ref[:, :rank, :].reshape(count * rank, -1)
    out_ref[...] = dot(right_ref[...].reshape(count * rank, part), mids, TN).astype(BF)


def product_of(message, received):
    count, rows, extra = message.shape
    _, rank, columns = received.shape
    part = columns - extra
    return pl.pallas_call(
        product_kernel,
        grid=(1,),
        in_specs=[
            pl.BlockSpec((count, rows, extra), lambda i: (0, 0, 0)),
            pl.BlockSpec((count, rank, part), lambda i: (0, 0, 0)),
        ],
        out_specs=pl.BlockSpec((part, extra), lambda i: (0, 0)),
        out_shape=jax.ShapeDtypeStruct((part, extra), BF),
        compiler_params=PARAMS,
    )(message, received)


def scale_kernel(product_ref, inverse_ref, out_ref):
    inverse = inverse_ref[...]
    high = inverse.astype(BF)
    low = (inverse - high.astype(F32)).astype(BF)
    product = product_ref[...]
    out_ref[...] = (dot(product, high, NT) + dot(product, low, NT)).astype(BF)


def weight_right_of(product, inverse):
    return pl.pallas_call(
        scale_kernel,
        out_shape=jax.ShapeDtypeStruct(product.shape, BF),
        compiler_params=PARAMS,
    )(product, inverse)


def to_chip(m):
    size = lax.axis_size("dp")
    return [(d, d ^ (2 * m)) for d in range(size)]


def swap_cores(value):
    return lax.ppermute(value, "dp", [(d, d ^ 1) for d in range(lax.axis_size("dp"))])


def after(value, *others):
    return lax.optimization_barrier((value, *others))[0]


def body(
    section_input, boundary_grad, carry_error, act_basis, weight_basis, outside_left, outside_right
):
    sections, parts = lax.axis_size("section"), lax.axis_size("dp")
    down = [(s, (s - 1) % sections) for s in range(sections)]
    up = [(s, (s + 1) % sections) for s in range(sections)]
    chips = parts // 2

    beyond = outside_right[0].T
    step = sections // 4
    group = jnp.stack(
        [beyond]
        + [
            lax.ppermute(beyond, "section", [(s + t, s) for s in range(0, sections, step)])
            for t in range(1, step)
        ]
    )
    basis_w = lax.ppermute(weight_basis[0], "section", up)
    basis_a = act_basis[0].T
    own = [basis_a] + [lax.ppermute(basis_a, "dp", to_chip(m)) for m in range(1, chips)]
    basis_w = lax.all_gather(after(basis_w, group, *own[1:4]), "dp", axis=0)
    groups = [group] + [lax.ppermute(group, "section", [(u * step, 0)]) for u in range(1, 4)]
    part = first_terms(after(boundary_grad, groups[1]), carry_error, own[:4])
    own, part, groups = lax.optimization_barrier((own, part, groups))
    own = jnp.stack(own)
    other = swap_cores(own)
    left, left_t = act_left(boundary_grad, carry_error, part, 4, own, other)
    recv_left = lax.ppermute(left_t, "section", down)
    cores = core_of(section_input, recv_left, outside_left.T, parts)
    new_error, right = act_right(boundary_grad, carry_error, left, left_t, parts)
    inner, message = inner_of(after(right, cores), basis_w, groups)
    cores = lax.all_to_all(cores, "dp", 0, 0)
    message = with_inner(message, lax.ppermute(inner, "section", down))
    received = lax.all_to_all(after(message, cores), "dp", 0, 0)

    left_sum, message = local_sum(cores, received)
    mid, gram = reduced(lax.all_to_all(message, "dp", 0, 0))
    mid = lax.ppermute(mid, "section", up)
    message = lax.all_to_all(copies_of(mid, gram, parts), "dp", 0, 0)
    product = lax.ppermute(product_of(message, received), "section", down)
    weight_left, inverse = weight_left_of(left_sum, message)
    weight_right = weight_right_of(product, inverse)
    return (new_error, weight_left[None], weight_right[None])


def solution(mesh):
    return jax.shard_map(
        body,
        mesh=mesh,
        in_specs=(
            P("section", "dp", None),
            P("section", "dp", None),
            P("section", "dp", None),
            P("section", "dp", None),
            P("section", "dp", None),
            P("dp", None),
            P("dp", "section", None),
        ),
        out_specs=(P("section", "dp", None), P("section", "dp", None), P("section", "dp", None)),
        check_vma=False,
    )
```

time: 236 us -> 174 us (0.74)
  waiting for transfers between devices: 58.5 us -> 32.8 us
  Pallas kernels: 42.6 us -> 25.2 us
  blocking collectives: 66 us -> 53.5 us
  starting transfers between devices: 37.9 us -> 33.8 us
    ppermute x17, waiting for transfers between devices: 37.1 us -> 22.1 us  [the longest x7 7.62 us: body(): lax.ppermute(basis_a, 'dp', to_chip(m))]
    all_to_all x3 -> x2, blocking collectives: 54.1 us -> 41.6 us  [the longest x1 28.4 us: body(): received = lax.all_to_all(after(message, cores), 'dp', 0, 0)]
    pallas_call x1, Pallas kernels: 12.9 us -> 4.93 us  [weight_left_of(): pl.pallas_call(left_kernel, out_shape=[jax.ShapeDtypeStruct((part, extra)...]
    ppermute x1, waiting for transfers between devices: 10.1 us -> 2.89 us  [body(): basis_w = lax.ppermute(weight_basis[0], 'section', up)]
    all_to_all x1 -> x0, waiting for transfers between devices: 7.24 us -> none  [spread(): return lax.all_to_all(copies, 'dp', 0, 0)]
    pallas_call x4 -> x7, Pallas kernels: 18.9 us -> 11.8 us  [the longest x1 3.68 us: inner_of(): pl.pallas_call(inner_kernel, grid=(steps,), in_specs=[pl.BlockSpec((block...]
    all_to_all x1 -> x0, starting transfers between devices: 5.63 us -> none  [spread(): return lax.all_to_all(copies, 'dp', 0, 0)]
    all_to_all x1, waiting for transfers between devices: 0.01 us -> 3.71 us  [body(): cores = lax.all_to_all(cores, 'dp', 0, 0)]
  transfers between devices with their start and end apart: 22 -> 21, of which waited for: 10 -> 12; matrix products, arithmetic and copies ran while one was open for 1% -> 1% of each run, Pallas kernels for 16% -> 12%
where the time goes in v2:
time: 174 us; the launch traced here: 173 us
  blocking collectives  53.5 us (31%)
  starting transfers between devices  33.8 us (19%)
  waiting for transfers between devices  32.8 us (19%)
  Pallas kernels  25.2 us (14%)
  between operations  14.3 us (8%)
  local copies, waits for them, and re-layouts  12.7 us (7%)
    all_to_all x1, blocking collectives, body(): received = lax.all_to_all(after(message, cores), 'dp', 0, 0)  28.4 us
    all_to_all x1, blocking collectives, body(): message = lax.all_to_all(copies_of(mid, gram, parts), 'dp', 0, 0)  13.2 us
    unnamed x37, local copies, waits for them, and re-layouts  12.6 us
    all_to_all x1, blocking collectives, body(): mid, gram = reduced(lax.all_to_all(message, 'dp', 0, 0))  11.9 us
    ppermute x7, starting transfers between devices, body(): lax.ppermute(basis_a, 'dp', to_chip(m))  9.4 us
    ppermute x7, waiting for transfers between devices, body(): lax.ppermute(basis_a, 'dp', to_chip(m))  7.62 us
    all_to_all x1, starting transfers between devices, body(): cores = lax.all_to_all(cores, 'dp', 0, 0)  7.16 us
    ppermute x1, waiting for transfers between devices, body(): mid = lax.ppermute(mid, 'section', up)  6.18 us
  transfers between devices with their start and end apart: 21, of which 12 were waited for; matrix products, arithmetic and copies ran while one was open for 1% of the time, Pallas kernels for 12%

profile of v2, /device:TPU:1, one launch (start us, length us, event | category | flops | bytes accessed | tf_op | source)
XLA Modules:
  0.0 173.2 jit_solution(14415381051761543232)
XLA Ops:
  7.2 0.0 all-gather.3.cloned.1.call-start
  7.2 1.3 collective-permute-start.8
  8.5 1.3 collective-permute-start.7
  9.8 1.3 collective-permute-start.9
  11.1 3.0 %collective-permute-start.15 = (bf16[768,128]{1,0:T(8,128)(2,1)}, bf16[768,128]{1,0:T(8,128)(2,1)S(1)}, u32[]{:S(2)}, u32[]{:S(2)}) collective-permute-start(bf16[768,128]{1,0:T(8,128)(2,1)} %bitcast.51), channel_id=1, source_target_pairs={{0,16},{16,32},{32,48},{48,64},{64,80},{80,96},{96,112},{112,128},... | collective-permute-start | bytes 589832 | tf_op jit(solution)/shard_map/ppermute | solution.py:440
  14.1 3.6 %collective-permute-start.2 = (bf16[64,768]{1,0:T(8,128)(2,1)}, bf16[64,768]{1,0:T(8,128)(2,1)S(1)}, u32[]{:S(2)}, u32[]{:S(2)}) collective-permute-start(bf16[64,768]{1,0:T(8,128)(2,1)} %bitcast.32), channel_id=1, source_target_pairs={{0,6},{1,7},{2,4},{3,5},{4,2},{5,3},{6,0},{7,1},{8,14},{9,15},{10,... | collective-permute-start | bytes 294920 | tf_op jit(solution)/shard_map/ppermute | solution.py:442
  17.7 0.3 collective-permute-start.1
  18.1 0.2 collective-permute-start
  18.3 0.9 pad_maximum_fusion.refs_0_
  19.3 1.6 collective-permute-done.2.refs_3_
  20.8 2.1 %collective-permute-done.1.refs_2_ = bf16[64,768]{1,0:T(8,128)(2,1)S(1)} collective-permute-done((bf16[64,768]{1,0:T(8,128)(2,1)}, bf16[64,768]{1,0:T(8,128)(2,1)S(1)}, u32[]{:S(2)}, u32[]{:S(2)}) %collective-permute-start.1) | collective-permute-done | bytes 98336 | tf_op jit(solution)/shard_map/ppermute | solution.py:442
  23.0 0.0 collective-permute-done.refs_1_
  23.0 2.9 %collective-permute-done.15 = bf16[768,128]{1,0:T(8,128)(2,1)S(1)} collective-permute-done((bf16[768,128]{1,0:T(8,128)(2,1)}, bf16[768,128]{1,0:T(8,128)(2,1)S(1)}, u32[]{:S(2)}, u32[]{:S(2)}) %collective-permute-start.15) | collective-permute-done | bytes 196640 | tf_op jit(solution)/shard_map/ppermute | solution.py:440
  25.9 0.7 copy-done.14
  26.5 0.0 all-gather.3.cloned.1.call-update
  26.6 1.3 collective-permute-start.10
  27.9 1.3 collective-permute-start.12
  29.2 1.3 collective-permute-start.11
  30.5 3.7 %collective-permute-start.6 = (bf16[64,768]{1,0:T(8,128)(2,1)}, bf16[64,768]{1,0:T(8,128)(2,1)S(1)}, u32[]{:S(2)}, u32[]{:S(2)}) collective-permute-start(bf16[64,768]{1,0:T(8,128)(2,1)} %bitcast.35), channel_id=1, source_target_pairs={{0,14},{1,15},{2,12},{3,13},{4,10},{5,11},{6,8},{7,9},{8,6},{9,7},... | collective-permute-start | bytes 294920 | tf_op jit(solution)/shard_map/ppermute | solution.py:442
  34.2 0.3 collective-permute-start.5
  34.5 2.2 %collective-permute-done.6 = bf16[64,768]{1,0:T(8,128)(2,1)S(1)} collective-permute-done((bf16[64,768]{1,0:T(8,128)(2,1)}, bf16[64,768]{1,0:T(8,128)(2,1)S(1)}, u32[]{:S(2)}, u32[]{:S(2)}) %collective-permute-start.6) | collective-permute-done | bytes 98336 | tf_op jit(solution)/shard_map/ppermute | solution.py:442
  36.7 0.6 collective-permute-start.4
  37.3 0.0 collective-permute-done.10.refs_1_
  37.4 0.8 copy-done.11
  38.1 0.6 collective-permute-start.3
  38.7 1.9 %copy-done = bf16[1,128,12288]{2,1,0:T(8,128)(2,1)S(1)} copy-done((bf16[1,128,12288]{2,1,0:T(8,128)(2,1)S(1)}, bf16[1,128,12288]{2,1,0:T(8,128)(2,1)}, u32[]{:S(2)}) %copy-start) | copy-done | bytes 3145752
  40.6 1.9 %copy-done.2 = bf16[1,128,12288]{2,1,0:T(8,128)(2,1)S(1)} copy-done((bf16[1,128,12288]{2,1,0:T(8,128)(2,1)S(1)}, bf16[1,128,12288]{2,1,0:T(8,128)(2,1)}, u32[]{:S(2)}) %copy-start.2) | copy-done | bytes 3145752
  42.5 0.9 copy-done.8
  43.4 0.6 shard_map.94.part_ref
  44.0 1.7 collective-permute-done.3
  45.7 3.7 %collective-permute-done.12.refs_3_ = bf16[4,64,768]{2,1,0:T(8,128)(2,1)S(1)} collective-permute-done((bf16[4,64,768]{2,1,0:T(8,128)(2,1)S(1)}, bf16[4,64,768]{2,1,0:T(8,128)(2,1)S(1)}, u32[]{:S(2)}, u32[]{:S(2)}) %collective-permute-start.12) | collective-permute-done | bytes 393248 | tf_op jit(solution)/shard_map/ppermute | solution.py:444
  49.5 0.7 copy-done.12
  50.1 0.1 copy-done.13
  50.3 2.6 %collective-permute-start.13 = (bf16[8,64,768]{2,1,0:T(8,128)(2,1)S(1)}, bf16[8,64,768]{2,1,0:T(8,128)(2,1)S(1)}, u32[]{:S(2)}, u32[]{:S(2)}) collective-permute-start(bf16[8,64,768]{2,1,0:T(8,128)(2,1)S(1)} %bitcast_dynamic-update-slice_fusion.own_ref), channel_id=1, source_target_pairs={{0,1},{1,0},{2,3},{3,2},{4,5},{5,4},{6,7},{7,6},{8,9},{9,8},{10,11... | collective-permute-start | bytes 2359304 | tf_op jit(solution)/shard_map/ppermute | solution.py:416
  52.8 1.9 %collective-permute-done.13.other_ref = bf16[8,64,768]{2,1,0:T(8,128)(2,1)S(1)} collective-permute-done((bf16[8,64,768]{2,1,0:T(8,128)(2,1)S(1)}, bf16[8,64,768]{2,1,0:T(8,128)(2,1)S(1)}, u32[]{:S(2)}, u32[]{:S(2)}) %collective-permute-start.13) | collective-permute-done | bytes 786464 | tf_op jit(solution)/shard_map/ppermute | solution.py:416
  54.7 3.6 %shard_map.95 = (bf16[128,64]{1,0:T(8,128)(2,1)S(1)}, bf16[64,128]{1,0:T(8,128)(2,1)S(1)}) custom-call(bf16[1,128,12288]{2,1,0:T(8,128)(2,1)S(1)} %copy-done, bf16[1,128,12288]{2,1,0:T(8,128)(2,1)S(1)} %copy-done.2, f32[128,64]{1,0:T(8,128)S(1)} %shard_map.94.part_ref, bf16[8,64,768]{2,1,0:T(8,128)(2,1)S(1)} %bitcast_dynamic-update-slice_fusion.own_ref, ...), custom_call_target="tpu_custom_call" | custom-call | tf_op jit(solution)/shard_map/pallas_call | solution.py:103
  58.3 0.1 collective-permute-start.14
  58.4 4.1 %collective-permute-done.14.left_t_ref = bf16[64,128]{1,0:T(8,128)(2,1)S(1)} collective-permute-done((bf16[64,128]{1,0:T(8,128)(2,1)S(1)}, bf16[64,128]{1,0:T(8,128)(2,1)S(1)}, u32[]{:S(2)}, u32[]{:S(2)}) %collective-permute-start.14) | collective-permute-done | bytes 16416 | tf_op jit(solution)/shard_map/ppermute | solution.py:450
  62.5 1.9 %shard_map.97 = bf16[16,64,768]{2,1,0:T(8,128)(2,1)S(1)} custom-call(bf16[1,128,12288]{2,1,0:T(8,128)(2,1)S(1)} %copy-done.5, bf16[64,128]{1,0:T(8,128)(2,1)S(1)} %collective-permute-done.14.left_t_ref, bf16[64,128]{1,0:T(8,128)(2,1)S(1)} %bitcast.41), custom_call_target="tpu_custom_call" | custom-call | tf_op jit(solution)/shard_map/pallas_call | solution.py:158
  64.4 1.2 copy-done.4
  65.6 7.2 %all-to-all-start = ((bf16[16,64,768]{2,1,0:T(8,128)(2,1)}), bf16[16,64,768]{2,1,0:T(8,128)(2,1)}, u32[]{:S(2)}, u32[]{:S(2)}) async-start(bf16[16,64,768]{2,1,0:T(8,128)(2,1)} %copy-done.4), calls=%async_computation | async-start | bytes 3145728 | tf_op jit(solution)/shard_map/all_to_all | solution.py:454
  72.8 0.0 copy-start.3
  72.8 1.9 %copy-done.3 = bf16[1,128,12288]{2,1,0:T(8,128)(2,1)S(1)} copy-done((bf16[1,128,12288]{2,1,0:T(8,128)(2,1)S(1)}, bf16[1,128,12288]{2,1,0:T(8,128)(2,1)}, u32[]{:S(2)}) %copy-start.3) | copy-done | bytes 3145752
  74.7 5.6 %shard_map.96 = (bf16[1,128,12288]{2,1,0:T(8,128)(2,1)}, bf16[16,64,768]{2,1,0:T(8,128)(2,1)S(1)}) custom-call(bf16[1,128,12288]{2,1,0:T(8,128)(2,1)S(1)} %copy-done.1, bf16[1,128,12288]{2,1,0:T(8,128)(2,1)S(1)} %copy-done.3, bf16[128,64]{1,0:T(8,128)(2,1)S(1)} %get-tuple-element.42.left_ref, bf16[64,128]{1,0:T(8,128)(2,1)S(1)} %get-tuple-element.43.left_t_ref), custom_call_target="tpu_custom_call" | custom-call | tf_op jit(solution)/shard_map/pallas_call | solution.py:126
  80.3 1.2 copy-done.6
  81.5 1.4 copy-done.7
  82.9 3.7 %shard_map.98 = (bf16[64,128]{1,0:T(8,128)(2,1)S(1)}, bf16[16,64,896]{2,1,0:T(8,128)(2,1)S(1)}) custom-call(bf16[16,64,768]{2,1,0:T(8,128)(2,1)S(1)} %copy-done.7, bf16[16,768,128]{2,1,0:T(8,128)(2,1)} %bitcast.42, bf16[4,64,768]{2,1,0:T(8,128)(2,1)} %copy-done.10, bf16[4,64,768]{2,1,0:T(8,128)(2,1)} %copy-done.11, bf16[4,64,768]{2,1,0:T(8,128)(2,1)} %copy-done.13, ...), custom_call_target="tpu_custom_call" | custom-call | tf_op jit(solution)/shard_map/pallas_call | solution.py:205
  86.6 2.7 %collective-permute-start.16 = (bf16[64,128]{1,0:T(8,128)(2,1)S(1)}, bf16[64,128]{1,0:T(8,128)(2,1)S(1)}, u32[]{:S(2)}, u32[]{:S(2)}) collective-permute-start(bf16[64,128]{1,0:T(8,128)(2,1)S(1)} %get-tuple-element.52), channel_id=1, source_target_pairs={{0,240},{16,0},{32,16},{48,32},{64,48},{80,64},{96,80},{112,96},{1... | collective-permute-start | bytes 49160 | tf_op jit(solution)/shard_map/ppermute | solution.py:455
  89.3 1.8 %collective-permute-done.16.inner_ref = bf16[64,128]{1,0:T(8,128)(2,1)S(1)} collective-permute-done((bf16[64,128]{1,0:T(8,128)(2,1)S(1)}, bf16[64,128]{1,0:T(8,128)(2,1)S(1)}, u32[]{:S(2)}, u32[]{:S(2)}) %collective-permute-start.16) | collective-permute-done | bytes 16416 | tf_op jit(solution)/shard_map/ppermute | solution.py:455
  91.1 0.2 shard_map.99
  91.3 3.7 %all-to-all-done.cores_ref = bf16[16,64,768]{2,1,0:T(8,128)(2,1)} async-done(((bf16[16,64,768]{2,1,0:T(8,128)(2,1)}), bf16[16,64,768]{2,1,0:T(8,128)(2,1)}, u32[]{:S(2)}, u32[]{:S(2)}) %all-to-all-start) | async-done | bytes 1572896 | tf_op jit(solution)/shard_map/all_to_all | solution.py:454
  95.0 28.4 %all_to_all.20.inner_ref.right_ref = bf16[16,64,896]{2,1,0:T(8,128)(2,1)S(1)} all-to-all(bf16[16,64,896]{2,1,0:T(8,128)(2,1)S(1)} %shard_map.99), channel_id=1, replica_groups=mesh['section'=16,'dp'=16] {'dp'}, dimensions={0} | all-to-all | bytes 3670016 | tf_op jit(solution)/shard_map/all_to_all | solution.py:456
  123.4 3.1 %shard_map.100 = (f32[128,768]{1,0:T(8,128)S(1)}, bf16[16,96,128]{2,1,0:T(8,128)(2,1)S(1)}) custom-call(bf16[16,64,768]{2,1,0:T(8,128)(2,1)} %all-to-all-done.cores_ref, bf16[16,64,896]{2,1,0:T(8,128)(2,1)S(1)} %all_to_all.20.inner_ref.right_ref), custom_call_target="tpu_custom_call" | custom-call | tf_op jit(solution)/shard_map/pallas_call | solution.py:281
  126.5 11.9 %all_to_all.21.received_ref = bf16[16,96,128]{2,1,0:T(8,128)(2,1)S(1)} all-to-all(bf16[16,96,128]{2,1,0:T(8,128)(2,1)S(1)} %get-tuple-element.56), channel_id=1, replica_groups=mesh['section'=16,'dp'=16] {'dp'}, dimensions={0} | all-to-all | bytes 786432 | tf_op jit(solution)/shard_map/all_to_all | solution.py:459
  138.4 0.1 shard_map.101
  138.4 0.1 collective-permute-start.17
  138.5 6.2 %collective-permute-done.17.mid_ref = bf16[64,128]{1,0:T(8,128)(2,1)S(1)} collective-permute-done((bf16[64,128]{1,0:T(8,128)(2,1)S(1)}, bf16[64,128]{1,0:T(8,128)(2,1)S(1)}, u32[]{:S(2)}, u32[]{:S(2)}) %collective-permute-start.17) | collective-permute-done | bytes 16416 | tf_op jit(solution)/shard_map/ppermute | solution.py:460
  144.7 0.1 shard_map.102
  144.8 13.2 %all_to_all.22.message_ref = bf16[16,96,128]{2,1,0:T(8,128)(2,1)S(1)} all-to-all(bf16[16,96,128]{2,1,0:T(8,128)(2,1)S(1)} %shard_map.102), channel_id=1, replica_groups=mesh['section'=16,'dp'=16] {'dp'}, dimensions={0} | all-to-all | bytes 786432 | tf_op jit(solution)/shard_map/all_to_all | solution.py:461
  158.0 0.6 shard_map.104
  158.6 1.0 collective-permute-start.18
  159.6 4.9 %shard_map.103 = (bf16[768,128]{1,0:T(8,128)(2,1)}, f32[128,128]{1,0:T(8,128)S(1)}) custom-call(f32[128,768]{1,0:T(8,128)S(1)} %get-tuple-element.55.left_sum_ref, bf16[16,96,128]{2,1,0:T(8,128)(2,1)S(1)} %all_to_all.22.message_ref), custom_call_target="tpu_custom_call" | custom-call | tf_op jit(solution)/shard_map/pallas_call | solution.py:361
  164.5 0.9 collective-permute-done.18.product_ref
  165.4 0.9 shard_map.105
  (33 shorter events, 0.1 us)
Async XLA Ops:
  7.2 74.3 %all-gather.3.cloned.1.call-start = ((), (), s32[]{:S(2)}) async-start(), calls=%async_computation.4 | async-start | bytes 3342336 | tf_op jit(solution)/shard_map/all_gather | solution.py:443
  7.2 10.5 %collective-permute-start.8 = (bf16[64,768]{1,0:T(8,128)(2,1)}, bf16[64,768]{1,0:T(8,128)(2,1)S(1)}, u32[]{:S(2)}, u32[]{:S(2)}) collective-permute-start(bf16[64,768]{1,0:T(8,128)(2,1)} %bitcast.44), channel_id=1, source_target_pairs={{32,0},{96,64},{160,128},{224,192},{33,1},{97,65},{161,129},{225,1... | collective-permute-start | bytes 294920 | tf_op jit(solution)/shard_map/ppermute | solution.py:436
  8.5 9.6 %collective-permute-start.7 = (bf16[64,768]{1,0:T(8,128)(2,1)}, bf16[64,768]{1,0:T(8,128)(2,1)S(1)}, u32[]{:S(2)}, u32[]{:S(2)}) collective-permute-start(bf16[64,768]{1,0:T(8,128)(2,1)} %bitcast.45), channel_id=1, source_target_pairs={{16,0},{80,64},{144,128},{208,192},{17,1},{81,65},{145,129},{209,1... | collective-permute-start | bytes 294920 | tf_op jit(solution)/shard_map/ppermute | solution.py:436
  9.8 8.5 %collective-permute-start.9 = (bf16[64,768]{1,0:T(8,128)(2,1)}, bf16[64,768]{1,0:T(8,128)(2,1)S(1)}, u32[]{:S(2)}, u32[]{:S(2)}) collective-permute-start(bf16[64,768]{1,0:T(8,128)(2,1)} %bitcast.46), channel_id=1, source_target_pairs={{48,0},{112,64},{176,128},{240,192},{49,1},{113,65},{177,129},{241... | collective-permute-start | bytes 294920 | tf_op jit(solution)/shard_map/ppermute | solution.py:436
  11.1 14.7 %collective-permute-start.15 = (bf16[768,128]{1,0:T(8,128)(2,1)}, bf16[768,128]{1,0:T(8,128)(2,1)S(1)}, u32[]{:S(2)}, u32[]{:S(2)}) collective-permute-start(bf16[768,128]{1,0:T(8,128)(2,1)} %bitcast.51), channel_id=1, source_target_pairs={{0,16},{16,32},{32,48},{48,64},{64,80},{80,96},{96,112},{112,128},... | collective-permute-start | bytes 589832 | tf_op jit(solution)/shard_map/ppermute | solution.py:440
  14.1 6.7 %collective-permute-start.2 = (bf16[64,768]{1,0:T(8,128)(2,1)}, bf16[64,768]{1,0:T(8,128)(2,1)S(1)}, u32[]{:S(2)}, u32[]{:S(2)}) collective-permute-start(bf16[64,768]{1,0:T(8,128)(2,1)} %bitcast.32), channel_id=1, source_target_pairs={{0,6},{1,7},{2,4},{3,5},{4,2},{5,3},{6,0},{7,1},{8,14},{9,15},{10,... | collective-permute-start | bytes 294920 | tf_op jit(solution)/shard_map/ppermute | solution.py:442
  17.7 5.3 %collective-permute-start.1 = (bf16[64,768]{1,0:T(8,128)(2,1)}, bf16[64,768]{1,0:T(8,128)(2,1)S(1)}, u32[]{:S(2)}, u32[]{:S(2)}) collective-permute-start(bf16[64,768]{1,0:T(8,128)(2,1)} %bitcast.33), channel_id=1, source_target_pairs={{0,4},{1,5},{2,6},{3,7},{4,0},{5,1},{6,2},{7,3},{8,12},{9,13},{10,... | collective-permute-start | bytes 294920 | tf_op jit(solution)/shard_map/ppermute | solution.py:442
  18.1 4.9 %collective-permute-start = (bf16[64,768]{1,0:T(8,128)(2,1)}, bf16[64,768]{1,0:T(8,128)(2,1)S(1)}, u32[]{:S(2)}, u32[]{:S(2)}) collective-permute-start(bf16[64,768]{1,0:T(8,128)(2,1)} %bitcast.34), channel_id=1, source_target_pairs={{0,2},{1,3},{2,0},{3,1},{4,6},{5,7},{6,4},{7,5},{8,10},{9,11},{10,... | collective-permute-start | bytes 294920 | tf_op jit(solution)/shard_map/ppermute | solution.py:442
  19.3 24.7 %copy-start.10 = (bf16[4,64,768]{2,1,0:T(8,128)(2,1)}, bf16[4,64,768]{2,1,0:T(8,128)(2,1)S(1)}, u32[]{:S(2)}) copy-start(bf16[4,64,768]{2,1,0:T(8,128)(2,1)S(1)} %pad_maximum_fusion.refs_0_) | copy-start | bytes 1179652
  25.9 0.7 copy-start.14
  26.6 10.8 %collective-permute-start.10 = (bf16[4,64,768]{2,1,0:T(8,128)(2,1)S(1)}, bf16[4,64,768]{2,1,0:T(8,128)(2,1)S(1)}, u32[]{:S(2)}, u32[]{:S(2)}) collective-permute-start(bf16[4,64,768]{2,1,0:T(8,128)(2,1)S(1)} %pad_maximum_fusion.refs_0_), channel_id=1, source_target_pairs={{64,0},{65,1},{66,2},{67,3},{68,4},{69,5},{70,6},{71,7},{72,8},{73... | collective-permute-start | bytes 1179656 | tf_op jit(solution)/shard_map/ppermute | solution.py:444
  27.9 21.5 %collective-permute-start.12 = (bf16[4,64,768]{2,1,0:T(8,128)(2,1)S(1)}, bf16[4,64,768]{2,1,0:T(8,128)(2,1)S(1)}, u32[]{:S(2)}, u32[]{:S(2)}) collective-permute-start(bf16[4,64,768]{2,1,0:T(8,128)(2,1)S(1)} %pad_maximum_fusion.refs_0_), channel_id=1, source_target_pairs={{192,0},{193,1},{194,2},{195,3},{196,4},{197,5},{198,6},{199,7},{2... | collective-permute-start | bytes 1179656 | tf_op jit(solution)/shard_map/ppermute | solution.py:444
  29.2 20.2 %collective-permute-start.11 = (bf16[4,64,768]{2,1,0:T(8,128)(2,1)S(1)}, bf16[4,64,768]{2,1,0:T(8,128)(2,1)S(1)}, u32[]{:S(2)}, u32[]{:S(2)}) collective-permute-start(bf16[4,64,768]{2,1,0:T(8,128)(2,1)S(1)} %pad_maximum_fusion.refs_0_), channel_id=1, source_target_pairs={{128,0},{129,1},{130,2},{131,3},{132,4},{133,5},{134,6},{135,7},{1... | collective-permute-start | bytes 1179656 | tf_op jit(solution)/shard_map/ppermute | solution.py:444
  30.5 6.3 %collective-permute-start.6 = (bf16[64,768]{1,0:T(8,128)(2,1)}, bf16[64,768]{1,0:T(8,128)(2,1)S(1)}, u32[]{:S(2)}, u32[]{:S(2)}) collective-permute-start(bf16[64,768]{1,0:T(8,128)(2,1)} %bitcast.35), channel_id=1, source_target_pairs={{0,14},{1,15},{2,12},{3,13},{4,10},{5,11},{6,8},{7,9},{8,6},{9,7},... | collective-permute-start | bytes 294920 | tf_op jit(solution)/shard_map/ppermute | solution.py:442
  34.2 9.7 %collective-permute-start.5 = (bf16[64,768]{1,0:T(8,128)(2,1)}, bf16[64,768]{1,0:T(8,128)(2,1)S(1)}, u32[]{:S(2)}, u32[]{:S(2)}) collective-permute-start(bf16[64,768]{1,0:T(8,128)(2,1)} %bitcast.36), channel_id=1, source_target_pairs={{0,12},{1,13},{2,14},{3,15},{4,8},{5,9},{6,10},{7,11},{8,4},{9,5},... | collective-permute-start | bytes 294920 | tf_op jit(solution)/shard_map/ppermute | solution.py:442
  36.7 7.2 %collective-permute-start.4 = (bf16[64,768]{1,0:T(8,128)(2,1)}, bf16[64,768]{1,0:T(8,128)(2,1)S(1)}, u32[]{:S(2)}, u32[]{:S(2)}) collective-permute-start(bf16[64,768]{1,0:T(8,128)(2,1)} %bitcast.37), channel_id=1, source_target_pairs={{0,10},{1,11},{2,8},{3,9},{4,14},{5,15},{6,12},{7,13},{8,2},{9,3},... | collective-permute-start | bytes 294920 | tf_op jit(solution)/shard_map/ppermute | solution.py:442
  37.4 0.8 copy-start.11
  38.1 7.6 %collective-permute-start.3 = (bf16[64,768]{1,0:T(8,128)(2,1)}, bf16[64,768]{1,0:T(8,128)(2,1)S(1)}, u32[]{:S(2)}, u32[]{:S(2)}) collective-permute-start(bf16[64,768]{1,0:T(8,128)(2,1)} %bitcast.38), channel_id=1, source_target_pairs={{0,8},{1,9},{2,10},{3,11},{4,12},{5,13},{6,14},{7,15},{8,0},{9,1},... | collective-permute-start | bytes 294920 | tf_op jit(solution)/shard_map/ppermute | solution.py:442
  38.7 1.9 %copy-start = (bf16[1,128,12288]{2,1,0:T(8,128)(2,1)S(1)}, bf16[1,128,12288]{2,1,0:T(8,128)(2,1)}, u32[]{:S(2)}) copy-start(bf16[1,128,12288]{2,1,0:T(8,128)(2,1)} %g_ref.4) | copy-start | bytes 9437188
  40.6 1.9 %copy-start.2 = (bf16[1,128,12288]{2,1,0:T(8,128)(2,1)S(1)}, bf16[1,128,12288]{2,1,0:T(8,128)(2,1)}, u32[]{:S(2)}) copy-start(bf16[1,128,12288]{2,1,0:T(8,128)(2,1)} %e_ref.5) | copy-start | bytes 9437188
  42.5 0.9 copy-start.8
  49.4 0.8 copy-start.12
  49.4 0.9 copy-start.13
  50.2 12.3 %copy-start.9 = (bf16[128,64]{0,1:T(8,128)(2,1)S(1)}, bf16[128,64]{0,1:T(8,128)(2,1)}, u32[]{:S(2)}) copy-start(bf16[128,64]{0,1:T(8,128)(2,1)} %param.12) | copy-start | bytes 49156
  50.3 4.5 %collective-permute-start.13 = (bf16[8,64,768]{2,1,0:T(8,128)(2,1)S(1)}, bf16[8,64,768]{2,1,0:T(8,128)(2,1)S(1)}, u32[]{:S(2)}, u32[]{:S(2)}) collective-permute-start(bf16[8,64,768]{2,1,0:T(8,128)(2,1)S(1)} %bitcast_dynamic-update-slice_fusion.own_ref), channel_id=1, source_target_pairs={{0,1},{1,0},{2,3},{3,2},{4,5},{5,4},{6,7},{7,6},{8,9},{9,8},{10,11... | collective-permute-start | bytes 2359304 | tf_op jit(solution)/shard_map/ppermute | solution.py:416
  54.7 7.8 %copy-start.5 = (bf16[1,128,12288]{2,1,0:T(8,128)(2,1)S(1)}, bf16[1,128,12288]{2,1,0:T(8,128)(2,1)}, u32[]{:S(2)}) copy-start(bf16[1,128,12288]{2,1,0:T(8,128)(2,1)} %x_ref.1) | copy-start | bytes 9437188
  58.3 4.2 %collective-permute-start.14 = (bf16[64,128]{1,0:T(8,128)(2,1)S(1)}, bf16[64,128]{1,0:T(8,128)(2,1)S(1)}, u32[]{:S(2)}, u32[]{:S(2)}) collective-permute-start(bf16[64,128]{1,0:T(8,128)(2,1)S(1)} %get-tuple-element.43.left_t_ref), channel_id=1, source_target_pairs={{0,240},{16,0},{32,16},{48,32},{64,48},{80,64},{96,80},{112,96},{1... | collective-permute-start | bytes 49160 | tf_op jit(solution)/shard_map/ppermute | solution.py:450
  64.4 1.2 copy-start.4
  65.6 7.2 %copy-start.1 = (bf16[1,128,12288]{2,1,0:T(8,128)(2,1)S(1)}, bf16[1,128,12288]{2,1,0:T(8,128)(2,1)}, u32[]{:S(2)}) copy-start(bf16[1,128,12288]{2,1,0:T(8,128)(2,1)} %g_ref.4) | copy-start | bytes 9437188
  65.6 29.4 %all-to-all-start = ((bf16[16,64,768]{2,1,0:T(8,128)(2,1)}), bf16[16,64,768]{2,1,0:T(8,128)(2,1)}, u32[]{:S(2)}, u32[]{:S(2)}) async-start(bf16[16,64,768]{2,1,0:T(8,128)(2,1)} %copy-done.4), calls=%async_computation | async-start | bytes 3145728 | tf_op jit(solution)/shard_map/all_to_all | solution.py:454
  72.8 1.9 %copy-start.3 = (bf16[1,128,12288]{2,1,0:T(8,128)(2,1)S(1)}, bf16[1,128,12288]{2,1,0:T(8,128)(2,1)}, u32[]{:S(2)}) copy-start(bf16[1,128,12288]{2,1,0:T(8,128)(2,1)} %e_ref.5) | copy-start | bytes 9437188
  80.3 1.2 copy-start.6
  81.5 1.4 copy-start.7
  86.6 4.5 %collective-permute-start.16 = (bf16[64,128]{1,0:T(8,128)(2,1)S(1)}, bf16[64,128]{1,0:T(8,128)(2,1)S(1)}, u32[]{:S(2)}, u32[]{:S(2)}) collective-permute-start(bf16[64,128]{1,0:T(8,128)(2,1)S(1)} %get-tuple-element.52), channel_id=1, source_target_pairs={{0,240},{16,0},{32,16},{48,32},{64,48},{80,64},{96,80},{112,96},{1... | collective-permute-start | bytes 49160 | tf_op jit(solution)/shard_map/ppermute | solution.py:455
  138.4 6.3 %collective-permute-start.17 = (bf16[64,128]{1,0:T(8,128)(2,1)S(1)}, bf16[64,128]{1,0:T(8,128)(2,1)S(1)}, u32[]{:S(2)}, u32[]{:S(2)}) collective-permute-start(bf16[64,128]{1,0:T(8,128)(2,1)S(1)} %get-tuple-element.57), channel_id=1, source_target_pairs={{0,16},{16,32},{32,48},{48,64},{64,80},{80,96},{96,112},{112,128},... | collective-permute-start | bytes 49160 | tf_op jit(solution)/shard_map/ppermute | solution.py:460
  158.6 6.8 %collective-permute-start.18 = (bf16[768,128]{1,0:T(8,128)(2,1)S(1)}, bf16[768,128]{1,0:T(8,128)(2,1)S(1)}, u32[]{:S(2)}, u32[]{:S(2)}) collective-permute-start(bf16[768,128]{1,0:T(8,128)(2,1)S(1)} %shard_map.104), channel_id=1, source_target_pairs={{0,240},{16,0},{32,16},{48,32},{64,48},{80,64},{96,80},{112,96},{1... | collective-permute-start | bytes 589832 | tf_op jit(solution)/shard_map/ppermute | solution.py:462
Sparse Core Ops, SparseCore 0:
  26.7 41.2 all-gather.2

commit v3 on v2

--- a/solution.py
+++ b/solution.py
@@ -141,26 +141,28 @@
     )(grad, error, left, left_t)
 
 
-def core_kernel(x_ref, left_t_ref, outside_ref, out_ref):
+def core_kernel(x_ref, left_t_ref, outside_ref, out_ref, blocks, sems):
     last = lax.axis_index("section") == lax.axis_size("section") - 1
     left_t = jnp.where(last, outside_ref[...].astype(F32), left_t_ref[...].astype(F32)).astype(BF)
-    core = dot(left_t, x_ref[...]).astype(BF)
     count, _, part = out_ref.shape
+    copies = []
     for i in range(count):
-        out_ref[i] = core[:, i * part : (i + 1) * part]
+        blocks[i] = dot(left_t, x_ref[0, :, i * part : (i + 1) * part]).astype(BF)
+        copies.append(pltpu.make_async_copy(blocks.at[i], out_ref.at[i], sems.at[i]))
+        copies[-1].start()
+    for copy in copies:
+        copy.wait()
 
 
 def core_of(inputs, left_t, outside_left_t, parts):
-    _, rows, width = inputs.shape
-    rank = left_t.shape[0]
-    steps = parts // 2
-    small = pl.BlockSpec((rank, rows), lambda m: (0, 0))
+    _, _, width = inputs.shape
+    shape = (parts, left_t.shape[0], width // parts)
     return pl.pallas_call(
         core_kernel,
-        grid=(steps,),
-        in_specs=[pl.BlockSpec((None, rows, width // steps), lambda m: (0, 0, m)), small, small],
-        out_specs=pl.BlockSpec((2, rank, width // parts), lambda m: (m, 0, 0)),
-        out_shape=jax.ShapeDtypeStruct((parts, rank, width // parts), BF),
+        in_specs=[pl.BlockSpec(memory_space=pltpu.VMEM)] * 3,
+        out_specs=pl.BlockSpec(memory_space=pltpu.HBM),
+        out_shape=jax.ShapeDtypeStruct(shape, BF),
+        scratch_shapes=[pltpu.VMEM(shape, BF), pltpu.SemaphoreType.DMA((parts,))],
         compiler_params=PARAMS,
     )(inputs, left_t, outside_left_t)
 
@@ -257,11 +259,23 @@
     return high, middle, (value - middle).astype(BF).astype(F32)
 
 
-def sum_kernel(cores_ref, inner_ref, left_sum_ref, message_ref):
+def sum_kernel(cores_ref, inner_ref, left_sum_ref, message_ref, cores, sems):
     count, rank, part = cores_ref.shape
-    cores_t = cores_ref[...].reshape(count * rank, part)
-    inner = inner_ref[...].reshape(count * rank, -1)
-    left_sum = dot(inner, cores_t, TN)
+    groups = sems.shape[0]
+    each = count // groups
+    copies = []
+    for i in range(groups):
+        where = pl.ds(i * each, each)
+        copies.append(pltpu.make_async_copy(cores_ref.at[where], cores.at[where], sems.at[i]))
+        copies[-1].start()
+    left_sum = None
+    for i, copy in enumerate(copies):
+        copy.wait()
+        block = cores[i * each : (i + 1) * each].reshape(each * rank, part)
+        inner = inner_ref[i * each : (i + 1) * each].reshape(each * rank, -1)
+        term = dot(inner, block, TN)
+        left_sum = term if left_sum is None else left_sum + term
+    cores_t = cores[...].reshape(count * rank, part)
     left_sum_ref[...] = left_sum
     high = left_sum.astype(BF)
     low = (left_sum - high.astype(F32)).astype(BF)
@@ -282,7 +296,7 @@
         sum_kernel,
         grid=(1,),
         in_specs=[
-            pl.BlockSpec((count, rank, part), lambda i: (0, 0, 0)),
+            pl.BlockSpec(memory_space=pltpu.HBM),
             pl.BlockSpec((count, rank, extra), lambda i: (0, 0, part // extra)),
         ],
         out_specs=[
@@ -293,6 +307,7 @@
             jax.ShapeDtypeStruct((extra, part), F32),
             jax.ShapeDtypeStruct((count, rank + 32, extra), BF),
         ],
+        scratch_shapes=[pltpu.VMEM(cores.shape, BF), pltpu.SemaphoreType.DMA((4,))],
         compiler_params=PARAMS,
     )(cores, received)
 

time: 174 us -> 177 us (1.017)
  Pallas kernels: 25.2 us -> 28.2 us
    pallas_call x2, Pallas kernels: 4.96 us -> 7.93 us  [the longest x1 4.88 us: core_of(): pl.pallas_call(core_kernel, in_specs=[pl.BlockSpec(memory_space=pltpu.VME...]
  transfers between devices with their start and end apart: 21 -> 21, of which waited for: 12 -> 12; matrix products, arithmetic and copies ran while one was open for 1% -> 1% of each run, Pallas kernels for 12% -> 13%
where the time goes in v3:
time: 177 us; the launch traced here: 176 us
  blocking collectives  53.5 us (30%)
  starting transfers between devices  33.4 us (19%)
  waiting for transfers between devices  33.2 us (19%)
  Pallas kernels  28.2 us (16%)
  between operations  14.3 us (8%)
  local copies, waits for them, and re-layouts  12.7 us (7%)
    all_to_all x1, blocking collectives, body(): received = lax.all_to_all(after(message, cores), 'dp', 0, 0)  28.4 us
    all_to_all x1, blocking collectives, body(): message = lax.all_to_all(copies_of(mid, gram, parts), 'dp', 0, 0)  13.2 us
    unnamed x37, local copies, waits for them, and re-layouts  12.6 us
    all_to_all x1, blocking collectives, body(): mid, gram = reduced(lax.all_to_all(message, 'dp', 0, 0))  11.9 us
    ppermute x7, starting transfers between devices, body(): lax.ppermute(basis_a, 'dp', to_chip(m))  9.4 us
    ppermute x7, waiting for transfers between devices, body(): lax.ppermute(basis_a, 'dp', to_chip(m))  7.62 us
    all_to_all x1, starting transfers between devices, body(): cores = lax.all_to_all(cores, 'dp', 0, 0)  7.16 us
    ppermute x1, waiting for transfers between devices, body(): mid = lax.ppermute(mid, 'section', up)  6.19 us
  transfers between devices with their start and end apart: 21, of which 12 were waited for; matrix products, arithmetic and copies ran while one was open for 1% of the time, Pallas kernels for 13%

profile of v3, /device:TPU:1, one launch (start us, length us, event | category | flops | bytes accessed | tf_op | source)
XLA Modules:
  0.0 176.2 jit_solution(4648458184414464199)
XLA Ops:
  7.2 0.0 all-gather.3.cloned.1.call-start
  7.2 1.3 collective-permute-start.8
  8.5 1.3 collective-permute-start.7
  9.8 1.3 collective-permute-start.9
  11.1 3.0 %collective-permute-start.15 = (bf16[768,128]{1,0:T(8,128)(2,1)}, bf16[768,128]{1,0:T(8,128)(2,1)S(1)}, u32[]{:S(2)}, u32[]{:S(2)}) collective-permute-start(bf16[768,128]{1,0:T(8,128)(2,1)} %bitcast.51), channel_id=1, source_target_pairs={{0,16},{16,32},{32,48},{48,64},{64,80},{80,96},{96,112},{112,128},... | collective-permute-start | bytes 589832 | tf_op jit(solution)/shard_map/ppermute | solution.py:455
  14.1 3.6 %collective-permute-start.2 = (bf16[64,768]{1,0:T(8,128)(2,1)}, bf16[64,768]{1,0:T(8,128)(2,1)S(1)}, u32[]{:S(2)}, u32[]{:S(2)}) collective-permute-start(bf16[64,768]{1,0:T(8,128)(2,1)} %bitcast.32), channel_id=1, source_target_pairs={{0,6},{1,7},{2,4},{3,5},{4,2},{5,3},{6,0},{7,1},{8,14},{9,15},{10,... | collective-permute-start | bytes 294920 | tf_op jit(solution)/shard_map/ppermute | solution.py:457
  17.7 0.0 collective-permute-done.8
  17.7 0.3 collective-permute-start.1
  18.1 0.0 collective-permute-done.7
  18.1 0.2 collective-permute-start
  18.3 0.9 pad_maximum_fusion.refs_0_
  19.3 1.6 collective-permute-done.2.refs_3_
  20.8 2.1 %collective-permute-done.1.refs_2_ = bf16[64,768]{1,0:T(8,128)(2,1)S(1)} collective-permute-done((bf16[64,768]{1,0:T(8,128)(2,1)}, bf16[64,768]{1,0:T(8,128)(2,1)S(1)}, u32[]{:S(2)}, u32[]{:S(2)}) %collective-permute-start.1) | collective-permute-done | bytes 98336 | tf_op jit(solution)/shard_map/ppermute | solution.py:457
  23.0 2.9 %collective-permute-done.15 = bf16[768,128]{1,0:T(8,128)(2,1)S(1)} collective-permute-done((bf16[768,128]{1,0:T(8,128)(2,1)}, bf16[768,128]{1,0:T(8,128)(2,1)S(1)}, u32[]{:S(2)}, u32[]{:S(2)}) %collective-permute-start.15) | collective-permute-done | bytes 196640 | tf_op jit(solution)/shard_map/ppermute | solution.py:455
  25.9 0.7 copy-done.14
  26.5 0.0 all-gather.3.cloned.1.call-update
  26.6 1.3 collective-permute-start.10
  27.9 1.3 collective-permute-start.12
  29.2 1.3 collective-permute-start.11
  30.5 3.7 %collective-permute-start.6 = (bf16[64,768]{1,0:T(8,128)(2,1)}, bf16[64,768]{1,0:T(8,128)(2,1)S(1)}, u32[]{:S(2)}, u32[]{:S(2)}) collective-permute-start(bf16[64,768]{1,0:T(8,128)(2,1)} %bitcast.35), channel_id=1, source_target_pairs={{0,14},{1,15},{2,12},{3,13},{4,10},{5,11},{6,8},{7,9},{8,6},{9,7},... | collective-permute-start | bytes 294920 | tf_op jit(solution)/shard_map/ppermute | solution.py:457
  34.2 0.3 collective-permute-start.5
  34.5 2.2 %collective-permute-done.6 = bf16[64,768]{1,0:T(8,128)(2,1)S(1)} collective-permute-done((bf16[64,768]{1,0:T(8,128)(2,1)}, bf16[64,768]{1,0:T(8,128)(2,1)S(1)}, u32[]{:S(2)}, u32[]{:S(2)}) %collective-permute-start.6) | collective-permute-done | bytes 98336 | tf_op jit(solution)/shard_map/ppermute | solution.py:457
  36.7 0.6 collective-permute-start.4
  37.4 0.8 copy-done.11
  38.1 0.6 collective-permute-start.3
  38.7 1.9 %copy-done = bf16[1,128,12288]{2,1,0:T(8,128)(2,1)S(1)} copy-done((bf16[1,128,12288]{2,1,0:T(8,128)(2,1)S(1)}, bf16[1,128,12288]{2,1,0:T(8,128)(2,1)}, u32[]{:S(2)}) %copy-start) | copy-done | bytes 3145752
  40.6 1.9 %copy-done.2 = bf16[1,128,12288]{2,1,0:T(8,128)(2,1)S(1)} copy-done((bf16[1,128,12288]{2,1,0:T(8,128)(2,1)S(1)}, bf16[1,128,12288]{2,1,0:T(8,128)(2,1)}, u32[]{:S(2)}) %copy-start.2) | copy-done | bytes 3145752
  42.5 0.9 copy-done.8
  43.4 0.6 shard_map.94.part_ref
  44.0 1.7 collective-permute-done.3
  45.7 3.7 %collective-permute-done.12.refs_3_ = bf16[4,64,768]{2,1,0:T(8,128)(2,1)S(1)} collective-permute-done((bf16[4,64,768]{2,1,0:T(8,128)(2,1)S(1)}, bf16[4,64,768]{2,1,0:T(8,128)(2,1)S(1)}, u32[]{:S(2)}, u32[]{:S(2)}) %collective-permute-start.12) | collective-permute-done | bytes 393248 | tf_op jit(solution)/shard_map/ppermute | solution.py:459
  49.5 0.7 copy-done.12
  50.1 0.1 copy-done.13
  50.3 2.6 %collective-permute-start.13 = (bf16[8,64,768]{2,1,0:T(8,128)(2,1)S(1)}, bf16[8,64,768]{2,1,0:T(8,128)(2,1)S(1)}, u32[]{:S(2)}, u32[]{:S(2)}) collective-permute-start(bf16[8,64,768]{2,1,0:T(8,128)(2,1)S(1)} %bitcast_dynamic-update-slice_fusion.own_ref), channel_id=1, source_target_pairs={{0,1},{1,0},{2,3},{3,2},{4,5},{5,4},{6,7},{7,6},{8,9},{9,8},{10,11... | collective-permute-start | bytes 2359304 | tf_op jit(solution)/shard_map/ppermute | solution.py:431
  52.8 1.9 %collective-permute-done.13.other_ref = bf16[8,64,768]{2,1,0:T(8,128)(2,1)S(1)} collective-permute-done((bf16[8,64,768]{2,1,0:T(8,128)(2,1)S(1)}, bf16[8,64,768]{2,1,0:T(8,128)(2,1)S(1)}, u32[]{:S(2)}, u32[]{:S(2)}) %collective-permute-start.13) | collective-permute-done | bytes 786464 | tf_op jit(solution)/shard_map/ppermute | solution.py:431
  54.7 3.6 %shard_map.95 = (bf16[128,64]{1,0:T(8,128)(2,1)S(1)}, bf16[64,128]{1,0:T(8,128)(2,1)S(1)}) custom-call(bf16[1,128,12288]{2,1,0:T(8,128)(2,1)S(1)} %copy-done, bf16[1,128,12288]{2,1,0:T(8,128)(2,1)S(1)} %copy-done.2, f32[128,64]{1,0:T(8,128)S(1)} %shard_map.94.part_ref, bf16[8,64,768]{2,1,0:T(8,128)(2,1)S(1)} %bitcast_dynamic-update-slice_fusion.own_ref, ...), custom_call_target="tpu_custom_call" | custom-call | tf_op jit(solution)/shard_map/pallas_call | solution.py:103
  58.3 0.1 collective-permute-start.14
  58.4 4.1 %collective-permute-done.14.left_t_ref = bf16[64,128]{1,0:T(8,128)(2,1)S(1)} collective-permute-done((bf16[64,128]{1,0:T(8,128)(2,1)S(1)}, bf16[64,128]{1,0:T(8,128)(2,1)S(1)}, u32[]{:S(2)}, u32[]{:S(2)}) %collective-permute-start.14) | collective-permute-done | bytes 16416 | tf_op jit(solution)/shard_map/ppermute | solution.py:465
  62.5 4.9 %shard_map.97 = bf16[16,64,768]{2,1,0:T(8,128)(2,1)S(1)} custom-call(bf16[1,128,12288]{2,1,0:T(8,128)(2,1)S(1)} %copy-done.5, bf16[64,128]{1,0:T(8,128)(2,1)S(1)} %collective-permute-done.14.left_t_ref, bf16[64,128]{1,0:T(8,128)(2,1)S(1)} %bitcast.41), custom_call_target="tpu_custom_call" | custom-call | tf_op jit(solution)/shard_map/pallas_call | solution.py:160
  67.4 1.2 copy-done.4
  68.6 7.2 %all-to-all-start = ((bf16[16,64,768]{2,1,0:T(8,128)(2,1)}), bf16[16,64,768]{2,1,0:T(8,128)(2,1)}, u32[]{:S(2)}, u32[]{:S(2)}) async-start(bf16[16,64,768]{2,1,0:T(8,128)(2,1)} %copy-done.4), calls=%async_computation | async-start | bytes 3145728 | tf_op jit(solution)/shard_map/all_to_all | solution.py:469
  75.8 0.0 copy-start.3
  75.8 1.9 %copy-done.3 = bf16[1,128,12288]{2,1,0:T(8,128)(2,1)S(1)} copy-done((bf16[1,128,12288]{2,1,0:T(8,128)(2,1)S(1)}, bf16[1,128,12288]{2,1,0:T(8,128)(2,1)}, u32[]{:S(2)}) %copy-start.3) | copy-done | bytes 3145752
  77.7 5.6 %shard_map.96 = (bf16[1,128,12288]{2,1,0:T(8,128)(2,1)}, bf16[16,64,768]{2,1,0:T(8,128)(2,1)S(1)}) custom-call(bf16[1,128,12288]{2,1,0:T(8,128)(2,1)S(1)} %copy-done.1, bf16[1,128,12288]{2,1,0:T(8,128)(2,1)S(1)} %copy-done.3, bf16[128,64]{1,0:T(8,128)(2,1)S(1)} %get-tuple-element.42.left_ref, bf16[64,128]{1,0:T(8,128)(2,1)S(1)} %get-tuple-element.43.left_t_ref), custom_call_target="tpu_custom_call" | custom-call | tf_op jit(solution)/shard_map/pallas_call | solution.py:126
  83.3 1.2 copy-done.6
  84.5 1.4 copy-done.7
  85.9 3.7 %shard_map.98 = (bf16[64,128]{1,0:T(8,128)(2,1)S(1)}, bf16[16,64,896]{2,1,0:T(8,128)(2,1)S(1)}) custom-call(bf16[16,64,768]{2,1,0:T(8,128)(2,1)S(1)} %copy-done.7, bf16[16,768,128]{2,1,0:T(8,128)(2,1)} %bitcast.42, bf16[4,64,768]{2,1,0:T(8,128)(2,1)} %copy-done.10, bf16[4,64,768]{2,1,0:T(8,128)(2,1)} %copy-done.11, bf16[4,64,768]{2,1,0:T(8,128)(2,1)} %copy-done.13, ...), custom_call_target="tpu_custom_call" | custom-call | tf_op jit(solution)/shard_map/pallas_call | solution.py:207
  89.6 2.5 %collective-permute-start.16 = (bf16[64,128]{1,0:T(8,128)(2,1)S(1)}, bf16[64,128]{1,0:T(8,128)(2,1)S(1)}, u32[]{:S(2)}, u32[]{:S(2)}) collective-permute-start(bf16[64,128]{1,0:T(8,128)(2,1)S(1)} %get-tuple-element.52), channel_id=1, source_target_pairs={{0,240},{16,0},{32,16},{48,32},{64,48},{80,64},{96,80},{112,96},{1... | collective-permute-start | bytes 49160 | tf_op jit(solution)/shard_map/ppermute | solution.py:470
  92.1 2.0 %collective-permute-done.16.inner_ref = bf16[64,128]{1,0:T(8,128)(2,1)S(1)} collective-permute-done((bf16[64,128]{1,0:T(8,128)(2,1)S(1)}, bf16[64,128]{1,0:T(8,128)(2,1)S(1)}, u32[]{:S(2)}, u32[]{:S(2)}) %collective-permute-start.16) | collective-permute-done | bytes 16416 | tf_op jit(solution)/shard_map/ppermute | solution.py:470
  94.1 0.2 shard_map.99
  94.3 3.7 %all-to-all-done.cores_ref = bf16[16,64,768]{2,1,0:T(8,128)(2,1)} async-done(((bf16[16,64,768]{2,1,0:T(8,128)(2,1)}), bf16[16,64,768]{2,1,0:T(8,128)(2,1)}, u32[]{:S(2)}, u32[]{:S(2)}) %all-to-all-start) | async-done | bytes 1572896 | tf_op jit(solution)/shard_map/all_to_all | solution.py:469
  98.0 28.4 %all_to_all.20.inner_ref.right_ref = bf16[16,64,896]{2,1,0:T(8,128)(2,1)S(1)} all-to-all(bf16[16,64,896]{2,1,0:T(8,128)(2,1)S(1)} %shard_map.99), channel_id=1, replica_groups=mesh['section'=16,'dp'=16] {'dp'}, dimensions={0} | all-to-all | bytes 3670016 | tf_op jit(solution)/shard_map/all_to_all | solution.py:471
  126.4 3.0 %shard_map.100 = (f32[128,768]{1,0:T(8,128)S(1)}, bf16[16,96,128]{2,1,0:T(8,128)(2,1)S(1)}) custom-call(bf16[16,64,768]{2,1,0:T(8,128)(2,1)} %all-to-all-done.cores_ref, bf16[16,64,896]{2,1,0:T(8,128)(2,1)S(1)} %all_to_all.20.inner_ref.right_ref), custom_call_target="tpu_custom_call" | custom-call | tf_op jit(solution)/shard_map/pallas_call | solution.py:295
  129.5 11.9 %all_to_all.21.received_ref = bf16[16,96,128]{2,1,0:T(8,128)(2,1)S(1)} all-to-all(bf16[16,96,128]{2,1,0:T(8,128)(2,1)S(1)} %get-tuple-element.56), channel_id=1, replica_groups=mesh['section'=16,'dp'=16] {'dp'}, dimensions={0} | all-to-all | bytes 786432 | tf_op jit(solution)/shard_map/all_to_all | solution.py:474
  141.4 0.1 shard_map.101
  141.4 0.1 collective-permute-start.17
  141.5 6.2 %collective-permute-done.17.mid_ref = bf16[64,128]{1,0:T(8,128)(2,1)S(1)} collective-permute-done((bf16[64,128]{1,0:T(8,128)(2,1)S(1)}, bf16[64,128]{1,0:T(8,128)(2,1)S(1)}, u32[]{:S(2)}, u32[]{:S(2)}) %collective-permute-start.17) | collective-permute-done | bytes 16416 | tf_op jit(solution)/shard_map/ppermute | solution.py:475
  147.7 0.1 shard_map.102
  147.8 13.2 %all_to_all.22.message_ref = bf16[16,96,128]{2,1,0:T(8,128)(2,1)S(1)} all-to-all(bf16[16,96,128]{2,1,0:T(8,128)(2,1)S(1)} %shard_map.102), channel_id=1, replica_groups=mesh['section'=16,'dp'=16] {'dp'}, dimensions={0} | all-to-all | bytes 786432 | tf_op jit(solution)/shard_map/all_to_all | solution.py:476
  161.0 0.6 shard_map.104
  161.6 0.8 collective-permute-start.18
  162.4 4.9 %shard_map.103 = (bf16[768,128]{1,0:T(8,128)(2,1)}, f32[128,128]{1,0:T(8,128)S(1)}) custom-call(f32[128,768]{1,0:T(8,128)S(1)} %get-tuple-element.55.left_sum_ref, bf16[16,96,128]{2,1,0:T(8,128)(2,1)S(1)} %all_to_all.22.message_ref), custom_call_target="tpu_custom_call" | custom-call | tf_op jit(solution)/shard_map/pallas_call | solution.py:376
  167.3 1.1 collective-permute-done.18.product_ref
  168.4 0.9 shard_map.105
  (33 shorter events, 0.1 us)
Async XLA Ops:
  7.2 77.3 %all-gather.3.cloned.1.call-start = ((), (), s32[]{:S(2)}) async-start(), calls=%async_computation.4 | async-start | bytes 3342336 | tf_op jit(solution)/shard_map/all_gather | solution.py:458
  7.2 10.5 %collective-permute-start.8 = (bf16[64,768]{1,0:T(8,128)(2,1)}, bf16[64,768]{1,0:T(8,128)(2,1)S(1)}, u32[]{:S(2)}, u32[]{:S(2)}) collective-permute-start(bf16[64,768]{1,0:T(8,128)(2,1)} %bitcast.44), channel_id=1, source_target_pairs={{32,0},{96,64},{160,128},{224,192},{33,1},{97,65},{161,129},{225,1... | collective-permute-start | bytes 294920 | tf_op jit(solution)/shard_map/ppermute | solution.py:451
  8.5 9.6 %collective-permute-start.7 = (bf16[64,768]{1,0:T(8,128)(2,1)}, bf16[64,768]{1,0:T(8,128)(2,1)S(1)}, u32[]{:S(2)}, u32[]{:S(2)}) collective-permute-start(bf16[64,768]{1,0:T(8,128)(2,1)} %bitcast.45), channel_id=1, source_target_pairs={{16,0},{80,64},{144,128},{208,192},{17,1},{81,65},{145,129},{209,1... | collective-permute-start | bytes 294920 | tf_op jit(solution)/shard_map/ppermute | solution.py:451
  9.8 8.5 %collective-permute-start.9 = (bf16[64,768]{1,0:T(8,128)(2,1)}, bf16[64,768]{1,0:T(8,128)(2,1)S(1)}, u32[]{:S(2)}, u32[]{:S(2)}) collective-permute-start(bf16[64,768]{1,0:T(8,128)(2,1)} %bitcast.46), channel_id=1, source_target_pairs={{48,0},{112,64},{176,128},{240,192},{49,1},{113,65},{177,129},{241... | collective-permute-start | bytes 294920 | tf_op jit(solution)/shard_map/ppermute | solution.py:451
  11.1 14.7 %collective-permute-start.15 = (bf16[768,128]{1,0:T(8,128)(2,1)}, bf16[768,128]{1,0:T(8,128)(2,1)S(1)}, u32[]{:S(2)}, u32[]{:S(2)}) collective-permute-start(bf16[768,128]{1,0:T(8,128)(2,1)} %bitcast.51), channel_id=1, source_target_pairs={{0,16},{16,32},{32,48},{48,64},{64,80},{80,96},{96,112},{112,128},... | collective-permute-start | bytes 589832 | tf_op jit(solution)/shard_map/ppermute | solution.py:455
  14.1 6.7 %collective-permute-start.2 = (bf16[64,768]{1,0:T(8,128)(2,1)}, bf16[64,768]{1,0:T(8,128)(2,1)S(1)}, u32[]{:S(2)}, u32[]{:S(2)}) collective-permute-start(bf16[64,768]{1,0:T(8,128)(2,1)} %bitcast.32), channel_id=1, source_target_pairs={{0,6},{1,7},{2,4},{3,5},{4,2},{5,3},{6,0},{7,1},{8,14},{9,15},{10,... | collective-permute-start | bytes 294920 | tf_op jit(solution)/shard_map/ppermute | solution.py:457
  17.7 5.3 %collective-permute-start.1 = (bf16[64,768]{1,0:T(8,128)(2,1)}, bf16[64,768]{1,0:T(8,128)(2,1)S(1)}, u32[]{:S(2)}, u32[]{:S(2)}) collective-permute-start(bf16[64,768]{1,0:T(8,128)(2,1)} %bitcast.33), channel_id=1, source_target_pairs={{0,4},{1,5},{2,6},{3,7},{4,0},{5,1},{6,2},{7,3},{8,12},{9,13},{10,... | collective-permute-start | bytes 294920 | tf_op jit(solution)/shard_map/ppermute | solution.py:457
  18.1 4.9 %collective-permute-start = (bf16[64,768]{1,0:T(8,128)(2,1)}, bf16[64,768]{1,0:T(8,128)(2,1)S(1)}, u32[]{:S(2)}, u32[]{:S(2)}) collective-permute-start(bf16[64,768]{1,0:T(8,128)(2,1)} %bitcast.34), channel_id=1, source_target_pairs={{0,2},{1,3},{2,0},{3,1},{4,6},{5,7},{6,4},{7,5},{8,10},{9,11},{10,... | collective-permute-start | bytes 294920 | tf_op jit(solution)/shard_map/ppermute | solution.py:457
  19.3 24.7 %copy-start.10 = (bf16[4,64,768]{2,1,0:T(8,128)(2,1)}, bf16[4,64,768]{2,1,0:T(8,128)(2,1)S(1)}, u32[]{:S(2)}) copy-start(bf16[4,64,768]{2,1,0:T(8,128)(2,1)S(1)} %pad_maximum_fusion.refs_0_) | copy-start | bytes 1179652
  25.9 0.7 copy-start.14
  26.6 10.8 %collective-permute-start.10 = (bf16[4,64,768]{2,1,0:T(8,128)(2,1)S(1)}, bf16[4,64,768]{2,1,0:T(8,128)(2,1)S(1)}, u32[]{:S(2)}, u32[]{:S(2)}) collective-permute-start(bf16[4,64,768]{2,1,0:T(8,128)(2,1)S(1)} %pad_maximum_fusion.refs_0_), channel_id=1, source_target_pairs={{64,0},{65,1},{66,2},{67,3},{68,4},{69,5},{70,6},{71,7},{72,8},{73... | collective-permute-start | bytes 1179656 | tf_op jit(solution)/shard_map/ppermute | solution.py:459
  27.9 21.5 %collective-permute-start.12 = (bf16[4,64,768]{2,1,0:T(8,128)(2,1)S(1)}, bf16[4,64,768]{2,1,0:T(8,128)(2,1)S(1)}, u32[]{:S(2)}, u32[]{:S(2)}) collective-permute-start(bf16[4,64,768]{2,1,0:T(8,128)(2,1)S(1)} %pad_maximum_fusion.refs_0_), channel_id=1, source_target_pairs={{192,0},{193,1},{194,2},{195,3},{196,4},{197,5},{198,6},{199,7},{2... | collective-permute-start | bytes 1179656 | tf_op jit(solution)/shard_map/ppermute | solution.py:459
  29.2 20.2 %collective-permute-start.11 = (bf16[4,64,768]{2,1,0:T(8,128)(2,1)S(1)}, bf16[4,64,768]{2,1,0:T(8,128)(2,1)S(1)}, u32[]{:S(2)}, u32[]{:S(2)}) collective-permute-start(bf16[4,64,768]{2,1,0:T(8,128)(2,1)S(1)} %pad_maximum_fusion.refs_0_), channel_id=1, source_target_pairs={{128,0},{129,1},{130,2},{131,3},{132,4},{133,5},{134,6},{135,7},{1... | collective-permute-start | bytes 1179656 | tf_op jit(solution)/shard_map/ppermute | solution.py:459
  30.5 6.3 %collective-permute-start.6 = (bf16[64,768]{1,0:T(8,128)(2,1)}, bf16[64,768]{1,0:T(8,128)(2,1)S(1)}, u32[]{:S(2)}, u32[]{:S(2)}) collective-permute-start(bf16[64,768]{1,0:T(8,128)(2,1)} %bitcast.35), channel_id=1, source_target_pairs={{0,14},{1,15},{2,12},{3,13},{4,10},{5,11},{6,8},{7,9},{8,6},{9,7},... | collective-permute-start | bytes 294920 | tf_op jit(solution)/shard_map/ppermute | solution.py:457
  34.2 9.7 %collective-permute-start.5 = (bf16[64,768]{1,0:T(8,128)(2,1)}, bf16[64,768]{1,0:T(8,128)(2,1)S(1)}, u32[]{:S(2)}, u32[]{:S(2)}) collective-permute-start(bf16[64,768]{1,0:T(8,128)(2,1)} %bitcast.36), channel_id=1, source_target_pairs={{0,12},{1,13},{2,14},{3,15},{4,8},{5,9},{6,10},{7,11},{8,4},{9,5},... | collective-permute-start | bytes 294920 | tf_op jit(solution)/shard_map/ppermute | solution.py:457
  36.7 7.2 %collective-permute-start.4 = (bf16[64,768]{1,0:T(8,128)(2,1)}, bf16[64,768]{1,0:T(8,128)(2,1)S(1)}, u32[]{:S(2)}, u32[]{:S(2)}) collective-permute-start(bf16[64,768]{1,0:T(8,128)(2,1)} %bitcast.37), channel_id=1, source_target_pairs={{0,10},{1,11},{2,8},{3,9},{4,14},{5,15},{6,12},{7,13},{8,2},{9,3},... | collective-permute-start | bytes 294920 | tf_op jit(solution)/shard_map/ppermute | solution.py:457
  37.4 0.8 copy-start.11
  38.1 7.6 %collective-permute-start.3 = (bf16[64,768]{1,0:T(8,128)(2,1)}, bf16[64,768]{1,0:T(8,128)(2,1)S(1)}, u32[]{:S(2)}, u32[]{:S(2)}) collective-permute-start(bf16[64,768]{1,0:T(8,128)(2,1)} %bitcast.38), channel_id=1, source_target_pairs={{0,8},{1,9},{2,10},{3,11},{4,12},{5,13},{6,14},{7,15},{8,0},{9,1},... | collective-permute-start | bytes 294920 | tf_op jit(solution)/shard_map/ppermute | solution.py:457
  38.7 1.9 %copy-start = (bf16[1,128,12288]{2,1,0:T(8,128)(2,1)S(1)}, bf16[1,128,12288]{2,1,0:T(8,128)(2,1)}, u32[]{:S(2)}) copy-start(bf16[1,128,12288]{2,1,0:T(8,128)(2,1)} %g_ref.4) | copy-start | bytes 9437188
  40.6 1.9 %copy-start.2 = (bf16[1,128,12288]{2,1,0:T(8,128)(2,1)S(1)}, bf16[1,128,12288]{2,1,0:T(8,128)(2,1)}, u32[]{:S(2)}) copy-start(bf16[1,128,12288]{2,1,0:T(8,128)(2,1)} %e_ref.5) | copy-start | bytes 9437188
  42.5 0.9 copy-start.8
  49.4 0.8 copy-start.12
  49.4 0.9 copy-start.13
  50.2 12.3 %copy-start.9 = (bf16[128,64]{0,1:T(8,128)(2,1)S(1)}, bf16[128,64]{0,1:T(8,128)(2,1)}, u32[]{:S(2)}) copy-start(bf16[128,64]{0,1:T(8,128)(2,1)} %param.12) | copy-start | bytes 49156
  50.3 4.5 %collective-permute-start.13 = (bf16[8,64,768]{2,1,0:T(8,128)(2,1)S(1)}, bf16[8,64,768]{2,1,0:T(8,128)(2,1)S(1)}, u32[]{:S(2)}, u32[]{:S(2)}) collective-permute-start(bf16[8,64,768]{2,1,0:T(8,128)(2,1)S(1)} %bitcast_dynamic-update-slice_fusion.own_ref), channel_id=1, source_target_pairs={{0,1},{1,0},{2,3},{3,2},{4,5},{5,4},{6,7},{7,6},{8,9},{9,8},{10,11... | collective-permute-start | bytes 2359304 | tf_op jit(solution)/shard_map/ppermute | solution.py:431
  54.7 7.8 %copy-start.5 = (bf16[1,128,12288]{2,1,0:T(8,128)(2,1)S(1)}, bf16[1,128,12288]{2,1,0:T(8,128)(2,1)}, u32[]{:S(2)}) copy-start(bf16[1,128,12288]{2,1,0:T(8,128)(2,1)} %x_ref.1) | copy-start | bytes 9437188
  58.3 4.2 %collective-permute-start.14 = (bf16[64,128]{1,0:T(8,128)(2,1)S(1)}, bf16[64,128]{1,0:T(8,128)(2,1)S(1)}, u32[]{:S(2)}, u32[]{:S(2)}) collective-permute-start(bf16[64,128]{1,0:T(8,128)(2,1)S(1)} %get-tuple-element.43.left_t_ref), channel_id=1, source_target_pairs={{0,240},{16,0},{32,16},{48,32},{64,48},{80,64},{96,80},{112,96},{1... | collective-permute-start | bytes 49160 | tf_op jit(solution)/shard_map/ppermute | solution.py:465
  67.4 1.2 copy-start.4
  68.6 7.2 %copy-start.1 = (bf16[1,128,12288]{2,1,0:T(8,128)(2,1)S(1)}, bf16[1,128,12288]{2,1,0:T(8,128)(2,1)}, u32[]{:S(2)}) copy-start(bf16[1,128,12288]{2,1,0:T(8,128)(2,1)} %g_ref.4) | copy-start | bytes 9437188
  68.6 29.4 %all-to-all-start = ((bf16[16,64,768]{2,1,0:T(8,128)(2,1)}), bf16[16,64,768]{2,1,0:T(8,128)(2,1)}, u32[]{:S(2)}, u32[]{:S(2)}) async-start(bf16[16,64,768]{2,1,0:T(8,128)(2,1)} %copy-done.4), calls=%async_computation | async-start | bytes 3145728 | tf_op jit(solution)/shard_map/all_to_all | solution.py:469
  75.8 1.9 %copy-start.3 = (bf16[1,128,12288]{2,1,0:T(8,128)(2,1)S(1)}, bf16[1,128,12288]{2,1,0:T(8,128)(2,1)}, u32[]{:S(2)}) copy-start(bf16[1,128,12288]{2,1,0:T(8,128)(2,1)} %e_ref.5) | copy-start | bytes 9437188
  83.3 1.2 copy-start.6
  84.5 1.4 copy-start.7
  89.6 4.5 %collective-permute-start.16 = (bf16[64,128]{1,0:T(8,128)(2,1)S(1)}, bf16[64,128]{1,0:T(8,128)(2,1)S(1)}, u32[]{:S(2)}, u32[]{:S(2)}) collective-permute-start(bf16[64,128]{1,0:T(8,128)(2,1)S(1)} %get-tuple-element.52), channel_id=1, source_target_pairs={{0,240},{16,0},{32,16},{48,32},{64,48},{80,64},{96,80},{112,96},{1... | collective-permute-start | bytes 49160 | tf_op jit(solution)/shard_map/ppermute | solution.py:470
  141.4 6.3 %collective-permute-start.17 = (bf16[64,128]{1,0:T(8,128)(2,1)S(1)}, bf16[64,128]{1,0:T(8,128)(2,1)S(1)}, u32[]{:S(2)}, u32[]{:S(2)}) collective-permute-start(bf16[64,128]{1,0:T(8,128)(2,1)S(1)} %get-tuple-element.57), channel_id=1, source_target_pairs={{0,16},{16,32},{32,48},{48,64},{64,80},{80,96},{96,112},{112,128},... | collective-permute-start | bytes 49160 | tf_op jit(solution)/shard_map/ppermute | solution.py:475
  161.6 6.8 %collective-permute-start.18 = (bf16[768,128]{1,0:T(8,128)(2,1)S(1)}, bf16[768,128]{1,0:T(8,128)(2,1)S(1)}, u32[]{:S(2)}, u32[]{:S(2)}) collective-permute-start(bf16[768,128]{1,0:T(8,128)(2,1)S(1)} %shard_map.104), channel_id=1, source_target_pairs={{0,240},{16,0},{32,16},{48,32},{64,48},{80,64},{96,80},{112,96},{1... | collective-permute-start | bytes 589832 | tf_op jit(solution)/shard_map/ppermute | solution.py:477
Sparse Core Ops, SparseCore 0:
  26.7 41.2 all-gather.2
